TPU v7x, 32 devices: a whole 2x2x4 slice. The times are simulated.
32 devices in a mesh: dp: 4 (over y, x), blk: 8 (over z, core).
Axes of the slice: x: 2, y: 2, z: 4, core: 2. Of those that a mesh axis runs over, the one named last changes fastest.
Arguments:
- tokens: bfloat16 [16, 2048, 512], P('dp', 'blk'), may hold values from -6 to 6
- teacher_tokens: bfloat16 [16, 2048, 512], P('dp', 'blk'), may hold values from -6 to 6
- segment_ids: int32 [16, 2048], P('dp', 'blk'), may hold values from 0 to 510, as said below
- cotangent: bfloat16 [16, 2048, 512], P('dp', 'blk'), may hold values from -6 to 6
- latent_qkv: bfloat16 [3, 512, 512], replicated, may hold values from -0.375 to 0.375
- latent_out: bfloat16 [512, 512], replicated, may hold values from -1.5 to 1.5
- latent_up: bfloat16 [512, 2048], replicated, may hold values from -0.25 to 0.25
- latent_down: bfloat16 [2048, 512], replicated, may hold values from -0.125 to 0.125
- student_gain: float32 [2, 512], replicated, may hold values from 0.25 to 1.75
- student_bias: float32 [6, 512], replicated, may hold values from -3 to 3
- student_up_bias: float32 [2048], replicated, may hold values from -3 to 3
- teacher_qkv: bfloat16 [3, 512, 512], P(None, 'dp'), may hold values from -0.375 to 0.375
- teacher_out: bfloat16 [512, 512], P('dp'), may hold values from -1.5 to 1.5
- teacher_up: bfloat16 [512, 2048], P('dp'), may hold values from -0.25 to 0.25
- teacher_down: bfloat16 [2048, 512], P('dp'), may hold values from -0.125 to 0.125
- teacher_gain: float32 [2, 512], replicated, may hold values from 0.25 to 1.75
- teacher_bias: float32 [6, 512], replicated, may hold values from -3 to 3
- teacher_up_bias: float32 [2048], replicated, may hold values from -3 to 3
Outputs:
- output: bfloat16 [16, 2048, 512], P('dp', 'blk')
- grad_tokens: bfloat16 [16, 2048, 512], P('dp', 'blk')
- grad_latent_qkv: float32 [3, 512, 512], replicated
- grad_latent_out: float32 [512, 512], replicated
- grad_latent_up: float32 [512, 2048], replicated
- grad_latent_down: float32 [2048, 512], replicated
- grad_student_gain: float32 [2, 512], replicated
- grad_student_bias: float32 [6, 512], replicated
- grad_student_up_bias: float32 [2048], replicated
Inputs may be any that keep to these rules, and one draw needn't show every extreme that they name: `segment_ids`: in each stream the ids start at 0 and never fall; one document of every stream begins within its first 256 tokens and ends within its last 256 tokens.
All inputs are finite; a program needn't handle non-finite values.
Results may differ from a plain program's by a relative error of at most 0.014.
Values may be sent and summed in bfloat16 or wider, within the bound.
A program may use at most 384 MiB of HBM per device.

v0:
```python
import functools

import jax
import jax.numpy as jnp
from jax import lax
from jax.experimental import pallas as pl
from jax.experimental.pallas import tpu as pltpu
from jax.sharding import PartitionSpec as P

HEADS = 8
BF = jnp.bfloat16
F32 = jnp.float32
LOG2E = 1.4426950408889634
clip_level = 2.5
masked_score = -1e30
VMEM_BYTES = 56 << 20
MESH = pl.DeviceIdType.MESH
NT = (((1,), (1,)), ((), ()))
TN = (((0,), (0,)), ((), ()))


def squash(tensor):
    return clip_level * jnp.tanh(tensor * (1.0 / clip_level))


def gelu_parts(tensor):
    phi = 0.5 * (1.0 + lax.erf(tensor * 0.7071067811865476))
    return tensor * phi, phi


def binarize(matrix):
    column_scale = jnp.sqrt(jnp.mean(matrix * matrix, axis=-2, keepdims=True) + 1e-06)
    return column_scale * jnp.tanh(2.0 * matrix / column_scale)


def layer_norm(tensor, gain_row, shift_row):
    centre = tensor - jnp.mean(tensor, axis=-1, keepdims=True)
    inverse_std = lax.rsqrt(jnp.mean(centre * centre, axis=-1, keepdims=True) + 1e-05)
    normed = centre * inverse_std
    return (normed * gain_row + shift_row, normed, inverse_std)


def norm_back(upstream, gain_row, normed, inverse_std):
    scaled = upstream * gain_row
    return inverse_std * (
        scaled
        - jnp.mean(scaled, axis=-1, keepdims=True)
        - normed * jnp.mean(scaled * normed, axis=-1, keepdims=True)
    )


def dot(a, b, dims=(((1,), (0,)), ((), ()))):
    return lax.dot_general(a, b, dims, preferred_element_type=F32)


def latent_grad(latent, binary_grad):
    matrix = latent.astype(F32)
    unused, pullback = jax.vjp(binarize, matrix)
    return pullback(binary_grad)[0]


def place(groups):
    here = lax.axis_index("blk")
    return here // groups, lax.rem(here, groups)


def greet(peers):
    barrier = pltpu.get_barrier_semaphore()
    for peer in peers:
        pl.semaphore_signal(barrier, inc=1, device_id=peer, device_id_type=MESH)
    pl.semaphore_wait(barrier, len(peers))


def stream_peers(streams, groups):
    s, r = place(groups)
    return [{"blk": lax.rem(s + d, streams) * groups + r} for d in range(1, streams)]


def core_peers(groups):
    s, r = place(groups)
    return [{"blk": s * groups + lax.rem(r + j, groups)} for j in range(1, groups)]


def dp_peers():
    size = lax.axis_size("dp")
    here = lax.axis_index("dp")
    return [{"dp": lax.rem(here + d, size)} for d in range(1, size)]


def unique(jobs):
    peers, kinds = [], []
    for job in jobs:
        for kind, found in job.peers():
            if kind not in kinds:
                kinds.append(kind)
                peers += found
    return peers


def remote(source, target, send, recv, peer):
    return pltpu.make_async_remote_copy(
        src_ref=source,
        dst_ref=target,
        send_sem=send,
        recv_sem=recv,
        device_id=peer,
        device_id_type=MESH,
    )


def dma(count):
    return pltpu.SemaphoreType.DMA((count,))


class Staged:
    def __init__(self, source, target, stage, sems):
        self.load = pltpu.make_async_copy(source, stage, sems.at[0])
        self.store = pltpu.make_async_copy(stage, target, sems.at[1])

    def first(self):
        self.load.start()

    def last(self):
        self.load.wait()
        self.store.start()
        self.store.wait()


class Gather:
    def __init__(self, streams, groups, block, dtype):
        self.streams, self.groups, self.block, self.dtype = streams, groups, block, dtype

    def scratch(self):
        b, g = self.streams, self.groups
        return [dma(b), dma(b), dma(b * g), dma(b * g), pltpu.VMEM(self.block, self.dtype), dma(2)]

    def out_shape(self):
        return jax.ShapeDtypeStruct((self.streams * self.groups,) + self.block, self.dtype)

    def peers(self):
        return [
            ("stream", stream_peers(self.streams, self.groups)),
            ("core", core_peers(self.groups)),
        ]

    def parts(self, source, target, send, recv, share_send, share_recv, stage, sems):
        b, g = self.streams, self.groups
        s, r = place(g)
        peers, cores = stream_peers(b, g), core_peers(g)
        swaps = [
            remote(
                source.at[lax.rem(s + d, b)],
                target.at[r * b + s],
                send.at[d],
                recv.at[d],
                peers[d - 1],
            )
            for d in range(1, b)
        ]
        shares = [
            [
                remote(
                    source.at[s] if d == 0 else target.at[r * b + lax.rem(s + b - d, b)],
                    target.at[r * b + lax.rem(s + b - d, b)],
                    share_send.at[j * b + d],
                    share_recv.at[j * b + d],
                    cores[j - 1],
                )
                for j in range(1, g)
            ]
            for d in range(b)
        ]
        own = Staged(source.at[s], target.at[r * b + s], stage, sems)
        return swaps, shares, own

    def first(self, *refs):
        swaps, shares, own = self.parts(*refs)
        for copy in swaps:
            copy.start()
        own.first()
        for copy in shares[0]:
            copy.start()

    def middle(self, *refs):
        swaps, shares, own = self.parts(*refs)
        for d in [1, 3, 2] if self.streams == 4 else range(1, self.streams):
            swaps[d - 1].wait_recv()
            for copy in shares[d]:
                copy.start()

    def last(self, *refs):
        swaps, shares, own = self.parts(*refs)
        own.last()
        for row in shares:
            for copy in row:
                copy.wait()
        for copy in swaps:
            copy.wait_send()


class Swap:
    def __init__(self, streams, groups, block, dtype):
        self.streams, self.groups, self.block, self.dtype = streams, groups, block, dtype

    def scratch(self):
        return [dma(self.streams), dma(self.streams), pltpu.VMEM(self.block, self.dtype), dma(2)]

    def out_shape(self):
        return jax.ShapeDtypeStruct((self.streams,) + self.block, self.dtype)

    def peers(self):
        return [("stream", stream_peers(self.streams, self.groups))]

    def parts(self, source, target, send, recv, stage, sems):
        b, g = self.streams, self.groups
        s, r = place(g)
        peers = stream_peers(b, g)
        swaps = [
            remote(source.at[lax.rem(s + d, b)], target.at[s], send.at[d], recv.at[d], peers[d - 1])
            for d in range(1, b)
        ]
        return swaps, Staged(source.at[s], target.at[s], stage, sems)

    def first(self, *refs):
        swaps, own = self.parts(*refs)
        for copy in swaps:
            copy.start()
        own.first()

    def last(self, *refs):
        swaps, own = self.parts(*refs)
        own.last()
        for copy in swaps:
            copy.wait()


class Spread:
    def __init__(self, block, dtype):
        self.block, self.dtype = block, dtype

    def scratch(self):
        size = lax.axis_size("dp")
        return [dma(size), dma(size), pltpu.VMEM(self.block, self.dtype), dma(2)]

    def out_shape(self):
        return jax.ShapeDtypeStruct((lax.axis_size("dp"),) + self.block, self.dtype)

    def peers(self):
        return [("dp", dp_peers())]

    def parts(self, source, target, send, recv, stage, sems):
        here = lax.axis_index("dp")
        copies = [
            remote(source, target.at[here], send.at[d], recv.at[d], peer)
            for d, peer in enumerate(dp_peers(), 1)
        ]
        return copies, Staged(source, target.at[here], stage, sems)

    first = Swap.first
    last = Swap.last


class Tiles:
    def __init__(self, bag, name, groups, pairs, per_owner):
        self.name, self.groups, self.pairs, self.per_owner = name, groups, pairs, per_owner
        count = pairs * per_owner
        bag.add(f"{name}_s", dma(groups * count))
        bag.add(f"{name}_r", dma(groups * count))

    def slot(self, who, pair, at):
        return (who * self.pairs + pair) * self.per_owner + at

    def copy(self, have, source, target, owner, pair, at):
        s, r = place(self.groups)
        return remote(
            source,
            target,
            have[f"{self.name}_s"].at[self.slot(owner, pair, at)],
            have[f"{self.name}_r"].at[self.slot(r, pair, at)],
            {"blk": s * self.groups + owner},
        )

    def own(self, have, source, target, pair, at):
        s, r = place(self.groups)
        return pltpu.make_async_copy(
            source, target, have[f"{self.name}_s"].at[self.slot(r, pair, at)]
        )

    def finish(self, have, source, target):
        s, r = place(self.groups)
        for pair in range(self.pairs):
            for at in range(self.per_owner):
                self.own(have, source, target, pair, at).wait()
                for j in range(1, self.groups):
                    other = lax.rem(r + j, self.groups)
                    remote(
                        source,
                        target,
                        have[f"{self.name}_s"].at[self.slot(other, pair, at)],
                        have[f"{self.name}_r"].at[self.slot(other, pair, at)],
                        {"blk": s * self.groups + other},
                    ).wait()


class Bag:
    def __init__(self):
        self.items = {}

    def add(self, name, item):
        self.items[name] = item

    def bind(self, refs):
        return dict(zip(self.items, refs))


class Reduce:
    def __init__(self, bag, name, streams, groups, shapes, over_cores, two_step):
        self.name, self.streams, self.groups = name, streams, groups
        self.size = lax.axis_size("dp")
        self.over_cores = over_cores
        self.two_step = two_step and self.size == 4 and streams % 2 == 0
        self.count = len(shapes)
        share = self.size * (groups if over_cores else 1)
        self.shapes = [(rows // share, cols) for rows, cols in shapes]
        self.wires = [BF if (c // streams) % 16 == 0 else F32 for c, cols in self.shapes]
        for i, (chunk, cols) in enumerate(self.shapes):
            wire, slim = self.wires[i], chunk // streams
            bag.add(f"{name}half{i}", pltpu.VMEM((self.size, chunk, cols), wire))
            if over_cores:
                bag.add(f"{name}core{i}", pltpu.VMEM((groups - 1, self.size, chunk, cols), wire))
            if self.two_step:
                bag.add(f"{name}first{i}", pltpu.VMEM((4, chunk // 2, cols), wire))
                bag.add(f"{name}second{i}", pltpu.VMEM((2, chunk // 2, cols), wire))
            else:
                bag.add(f"{name}dp{i}", pltpu.VMEM((self.size - 1, chunk, cols), wire))
            bag.add(f"{name}cut{i}", pltpu.VMEM((streams, slim, cols), wire))
            bag.add(f"{name}z{i}", pltpu.VMEM((streams - 1, slim, cols), wire))
            bag.add(f"{name}fin{i}", pltpu.VMEM((slim, cols), wire))
            for kind in self.kinds():
                bag.add(f"{name}{kind}s{i}", dma(self.sem_count(kind)))
                bag.add(f"{name}{kind}r{i}", dma(self.sem_count(kind)))
            bag.add(f"{name}local{i}", dma(2))

    def kinds(self):
        along = ["b1", "b2", "c", "d", "e1", "e2"] if self.two_step else ["b", "c", "d", "e"]
        return (["a"] if self.over_cores else []) + along + ["f"]

    def sem_count(self, kind):
        if kind in ("a", "f"):
            return self.groups
        if kind in ("c", "d"):
            return self.streams
        return max(self.size, 4)

    def out_shapes(self):
        return [
            jax.ShapeDtypeStruct(
                (self.groups, self.size, self.streams, chunk // self.streams, cols), wire
            )
            for (chunk, cols), wire in zip(self.shapes, self.wires)
        ]

    def bind(self, sources, targets, scratch):
        self.sources, self.targets, self.scratch = sources, targets, scratch

    def get(self, what, i):
        return self.scratch[f"{self.name}{what}{i}"]

    def pairs(self, kind, i):
        s, r = place(self.groups)
        here = lax.axis_index("dp")
        b, g, size = self.streams, self.groups, self.size
        x, y = lax.rem(here, 2), here // 2
        beside_x, beside_y = {"dp": 2 * y + 1 - x}, {"dp": 2 * (1 - y) + x}
        if kind == "a":
            for d, peer in enumerate(core_peers(g), 1):
                yield d, self.sources[i].at[lax.rem(r + d, g)], self.get("core", i).at[d - 1], peer
        elif kind == "b":
            half, box = self.get("half", i), self.get("dp", i)
            for d, peer in enumerate(dp_peers(), 1):
                yield d, half.at[lax.rem(here + d, size)], box.at[d - 1], peer
        elif kind == "b1":
            half, box, h = self.get("half", i), self.get("first", i), self.shapes[i][0] // 2
            for n in range(2):
                yield n, half.at[2 * n + 1 - x, pl.ds(0, h)], box.at[n], beside_x
                yield 2 + n, half.at[2 * (1 - y) + n, pl.ds(h, h)], box.at[2 + n], beside_y
        elif kind == "b2":
            half, box, h = self.get("half", i), self.get("second", i), self.shapes[i][0] // 2
            yield 0, half.at[2 * (1 - y) + x, pl.ds(0, h)], box.at[0], beside_y
            yield 1, half.at[2 * y + 1 - x, pl.ds(h, h)], box.at[1], beside_x
        elif kind in "cd":
            peers = list(enumerate(stream_peers(b, g), 1))
            for d, peer in [peers[1], peers[0], peers[2]] if b == 4 else peers:
                if kind == "c":
                    cut = self.get("cut", i)
                    yield d, cut.at[lax.rem(s + d, b)], self.get("z", i).at[d - 1], peer
                else:
                    yield d, self.get("fin", i), self.targets[i].at[r, here, s], peer
        elif kind == "e":
            whole = self.targets[i].at[r, here]
            for d, peer in enumerate(dp_peers(), 1):
                yield d, whole, whole, peer
        elif kind == "e1":
            for n, peer in enumerate((beside_y, beside_x)):
                part = self.targets[i].at[r, here, pl.ds(n * b // 2, b // 2)]
                yield n, part, part, peer
        elif kind == "e2":
            for n in range(2):
                part = self.targets[i].at[r, 2 * n + x, pl.ds(0, b // 2)]
                yield n, part, part, beside_x
                part = self.targets[i].at[r, 2 * y + n, pl.ds(b // 2, b // 2)]
                yield 2 + n, part, part, beside_y
        else:
            whole = self.targets[i].at[r]
            for d, peer in enumerate(core_peers(g), 1):
                yield d, whole, whole, peer

    def copies(self, kind, i):
        send, recv = self.get(kind + "s", i), self.get(kind + "r", i)
        for n, source, target, peer in self.pairs(kind, i):
            yield remote(source, target, send.at[n], recv.at[n], peer)

    def start(self, kind, i):
        for copy in self.copies(kind, i):
            copy.start()

    def arrive(self, kind, i):
        for copy in self.copies(kind, i):
            copy.wait_recv()

    def load(self, i):
        s, r = place(self.groups)
        return pltpu.make_async_copy(
            self.sources[i].at[r], self.get("half", i), self.get("local", i).at[0]
        )

    def keep(self, i):
        s, r = place(self.groups)
        return pltpu.make_async_copy(
            self.get("fin", i),
            self.targets[i].at[r, lax.axis_index("dp"), s],
            self.get("local", i).at[1],
        )

    def stages(self):
        middle = [self.dp_middle] if self.two_step else []
        back = [self.dp_back_middle] if self.two_step else []
        return [self.dp_start, *middle, self.z_start, self.z_back, self.dp_back, *back, self.core_back]

    def core_start(self):
        for i in range(self.count):
            self.start("a", i)
            self.load(i).start()

    def dp_start(self):
        for i in range(self.count):
            if self.over_cores:
                self.load(i).wait()
                self.arrive("a", i)
                half, box, wire = self.get("half", i), self.get("core", i), self.wires[i]
                for p in range(self.size):
                    total = half[p].astype(F32)
                    for j in range(self.groups - 1):
                        total = total + box[j, p].astype(F32)
                    half[p] = total.astype(wire)
            self.start("b1" if self.two_step else "b", i)

    def dp_middle(self):
        here = lax.axis_index("dp")
        x, y = lax.rem(here, 2), here // 2
        for i in range(self.count):
            self.arrive("b1", i)
            half, box, wire = self.get("half", i), self.get("first", i), self.wires[i]
            h = self.shapes[i][0] // 2
            for n in range(2):
                for who, at, part in ((2 * n + x, pl.ds(0, h), n), (2 * y + n, pl.ds(h, h), 2 + n)):
                    total = half[who, at, :].astype(F32) + box[part].astype(F32)
                    half[who, at, :] = total.astype(wire)
            self.start("b2", i)

    def z_start(self):
        here = lax.axis_index("dp")
        for i in range(self.count):
            self.arrive("b2" if self.two_step else "b", i)
            half, cut, wire = self.get("half", i), self.get("cut", i), self.wires[i]
            chunk = self.shapes[i][0]
            slim = chunk // self.streams
            for z in range(self.streams):
                at = slice(z * slim, (z + 1) * slim)
                total = half[here, at, :].astype(F32)
                if self.two_step:
                    which, first = divmod(z * slim, chunk // 2)
                    total = total + self.get("second", i)[which, first : first + slim].astype(F32)
                else:
                    for d in range(self.size - 1):
                        total = total + self.get("dp", i)[d, at, :].astype(F32)
                cut[z] = total.astype(wire)
            self.start("c", i)

    def z_back(self):
        s, r = place(self.groups)
        for i in range(self.count):
            self.arrive("c", i)
            box = self.get("z", i)
            total = self.get("cut", i)[s].astype(F32)
            for d in range(self.streams - 1):
                total = total + box[d].astype(F32)
            self.get("fin", i)[...] = total.astype(self.wires[i])
            self.keep(i).start()
            self.start("d", i)

    def dp_back(self):
        for i in range(self.count):
            self.keep(i).wait()
            self.arrive("d", i)
            self.start("e1" if self.two_step else "e", i)

    def dp_back_middle(self):
        for i in range(self.count):
            self.arrive("e1", i)
            self.start("e2", i)

    def core_back(self):
        for i in range(self.count):
            self.arrive("e2" if self.two_step else "e", i)
            self.start("f", i)

    def end(self):
        for i in range(self.count):
            self.arrive("f", i)
            for kind in self.kinds():
                for copy in self.copies(kind, i):
                    copy.wait_send()


class Moves:
    def __init__(self, *jobs, others=()):
        self.jobs, self.others = list(jobs), list(others)
        self.counts = [len(job.scratch()) for job in jobs]

    def scratch(self):
        return [item for job in self.jobs for item in job.scratch()]

    def out_shapes(self):
        return [job.out_shape() for job in self.jobs]

    def spaces(self):
        return [pl.BlockSpec(memory_space=pl.ANY)] * len(self.jobs)

    def each(self, sources, targets, scratch):
        at = 0
        for job, count, source, target in zip(self.jobs, self.counts, sources, targets):
            yield job, (source, target, *scratch[at : at + count])
            at += count

    def first(self, sources, targets, scratch, count=None):
        greet(unique(self.jobs + self.others))
        for job, refs in list(self.each(sources, targets, scratch))[:count]:
            job.first(*refs)

    def start_last(self, sources, targets, scratch):
        for job, refs in list(self.each(sources, targets, scratch))[-1:]:
            job.first(*refs)

    def middle(self, sources, targets, scratch):
        for job, refs in self.each(sources, targets, scratch):
            if isinstance(job, Gather):
                job.middle(*refs)

    def last(self, sources, targets, scratch):
        for job, refs in self.each(sources, targets, scratch):
            job.last(*refs)


def remote_params(collective_id):
    return pltpu.CompilerParams(
        collective_id=collective_id, has_side_effects=True, vmem_limit_bytes=VMEM_BYTES
    )


def binary_columns(latent):
    matrix = latent.astype(F32)
    scale = jnp.sqrt(jnp.mean(matrix * matrix, axis=0, keepdims=True) + 1e-06)
    return (scale * jnp.tanh(matrix * (2.0 / scale))).astype(BF)


def intake_kernel(moves, groups, *refs):
    count = len(moves.jobs)
    latents, ids_ref, refs = refs[:4], refs[4], refs[5:]
    sources, refs = refs[: count - 1], refs[count - 1 :]
    results, refs = refs[:4], refs[4:]
    targets, refs = refs[:count], refs[count:]
    loaded, made, sems = refs[:4], refs[4:8], refs[8]
    ids_in, ids_box, *scratch = refs[9:]
    sources = (*sources, ids_box)
    moves.first(sources, targets, scratch, count - 1)
    s, r = place(groups)
    width = results[0].shape[3]
    own = pl.ds(pl.multiple_of(r * width, 128), width)
    places = [latents[0].at[:, :, own], *latents[1:]]
    loads = [
        pltpu.make_async_copy(source, target, sems.at[i])
        for i, (source, target) in enumerate(zip(places, loaded))
    ]
    stores = [
        pltpu.make_async_copy(source, target, sems.at[4 + i])
        for i, (source, target) in enumerate(zip(made, [results[0].at[0], *results[1:]]))
    ]
    fetch = pltpu.make_async_copy(ids_ref, ids_in, sems.at[8])
    fetch.start()
    for copy in loads:
        copy.start()
    fetch.wait()
    ids = ids_in[...].astype(F32)
    for i in range(ids.shape[0]):
        ids_box[i] = jnp.broadcast_to(ids[i : i + 1, :], ids_box.shape[1:])
    moves.start_last(sources, targets, scratch)
    loads[0].wait()
    for i in range(3):
        made[0][i] = binary_columns(loaded[0][i])
    stores[0].start()
    for n in range(1, 4):
        loads[n].wait()
        for i in range(0, loaded[n].shape[1], 128):
            made[n][:, i : i + 128] = binary_columns(loaded[n][:, i : i + 128])
        stores[n].start()
    moves.middle(sources, targets, scratch)
    for copy in stores:
        copy.wait()
    moves.last(sources, targets, scratch)


def intake(moves, groups, latents, ids, arrays, collective_id):
    three, depth, unused = latents[0].shape
    own_shape = (three, depth, depth // groups)
    shapes = [(1,) + own_shape] + [a.shape for a in latents[1:]]
    buffers = [pltpu.VMEM(shape, BF) for shape in [own_shape] + shapes[1:]]
    any_space = [pl.BlockSpec(memory_space=pl.ANY)] * 4
    return pl.pallas_call(
        functools.partial(intake_kernel, moves, groups),
        out_shape=[jax.ShapeDtypeStruct(shape, BF) for shape in shapes] + moves.out_shapes(),
        in_specs=any_space
        + moves.spaces(),
        out_specs=any_space + moves.spaces(),
        scratch_shapes=buffers * 2
        + [dma(9), pltpu.VMEM(ids.shape, ids.dtype)]
        + [pltpu.VMEM((ids.shape[0], 8, ids.shape[1]), F32)]
        + moves.scratch(),
        compiler_params=remote_params(collective_id),
        name="intake",
    )(*latents, ids, *arrays)


def lanes_of(shape):
    return lax.broadcasted_iota(jnp.int32, shape, 1)


def forward_kernel(
    moves, keep, streams, groups, tile, bag, tiles, x_ref, w_ref, bias_ref, docs_ref, *rest
):
    count = len(moves.jobs)
    sources, rest = rest[:count], rest[count:]
    q_ref, k_ref, rows_ref, *rest = rest
    if keep:
        v_ref, e_ref, ctx_ref, inv_ref, active_ref, *rest = rest
    targets, rest = rest[:count], rest[count:]
    have = bag.bind(rest)
    scratch = tuple(have[f"moves{i}"] for i in range(len(moves.scratch())))
    k_aug, v_aug, ctx_all, mask, edges = (
        have["k_aug"],
        have["v_aug"],
        have["ctx_all"],
        have["mask"],
        have["edges"],
    )
    active = active_ref if keep else x_ref
    row_ref = have["row"]
    pair, step = pl.program_id(0), pl.program_id(1)
    pairs, steps = pl.num_programs(0), pl.num_programs(1)
    seq = k_ref.shape[0]
    s, r = place(groups)
    sub = min(256, tile)
    width = w_ref.shape[3]
    n_pairs = ctx_all.shape[0]
    offset = pair * 128 if width == n_pairs * 128 else (r * n_pairs + pair) * 128
    offset = pl.multiple_of(offset, 128)
    home = pl.multiple_of((r * n_pairs + pair) * 128, 128)

    @pl.when((pair == 0) & (step == 0))
    def _():
        moves.first(sources, targets, scratch)
        ids = stream_row(docs_ref)
        row_ref[...] = ids
        big_at = long_at(streams, groups, seq)
        big = ids[:, big_at : big_at + 1]
        mask[...] = jnp.where(ids == big, 0.0, masked_score)
        edges[0] = jnp.broadcast_to(ids[:, :sub], (128, sub)).T
        edges[1] = jnp.broadcast_to(ids[:, seq - sub :], (128, sub)).T
        if keep:
            for i in range(0, seq, 256):
                active_ref[i : i + 256, :] = squash(x_ref[i : i + 256, :].astype(F32)).astype(BF)

    @pl.when((pair == pairs - 1) & (step == steps - 2))
    def _():
        moves.middle(sources, targets, scratch)

    @pl.when(step == 0)
    def _():
        columns = pl.ds(offset, 128)

        def project(i, bias):
            matrix = jnp.concatenate(
                [w_ref[d, i, :, columns] for d in range(w_ref.shape[0])], axis=0
            )
            result = dot(active[...], matrix)
            if bias is not None:
                result = result + bias_ref[bias : bias + 1, pl.ds(home, 128)]
            return result.astype(BF)

        low = lanes_of((seq, 128)) < 64
        lane = lanes_of((seq, 128))
        q_ref[...] = (project(0, 0).astype(F32) * 0.125).astype(BF)
        keys = project(1, None)
        k_ref[...] = keys
        keys = keys.astype(F32)
        turned = pltpu.roll(keys, 64, 1)
        k_aug[0] = jnp.where(low, keys, turned).astype(BF)
        k_aug[1] = jnp.where(low, turned, keys).astype(BF)
        values = project(2, 1)
        if keep:
            v_ref[...] = values
        values = values.astype(F32)
        v_aug[0] = jnp.where(low, values, jnp.where(lane < 66, 1.0, 0.0)).astype(BF)
        v_aug[1] = jnp.where(low, jnp.where(lane < 2, 1.0, 0.0), values).astype(BF)

    turned = own_rows_last(step, seq, tile, groups)
    start = pl.multiple_of(turned * tile, tile)

    def body(edge_at):
        low = lanes_of((sub, 128)) < 64
        parts = []
        for at in range(0, tile, sub):
            scaled = q_ref[pl.ds(start + at, sub), :].astype(F32) * LOG2E
            upper = scaled.astype(BF).astype(F32)
            lower = scaled - upper
            parts.append(
                (
                    jnp.where(low, upper, pltpu.roll(lower, 64, 1)).astype(BF),
                    jnp.where(low, pltpu.roll(upper, 64, 1), lower).astype(BF),
                )
            )
        chains = [(at, h) for at in range(0, tile, sub) for h in range(2)]

        def scores_of(at, h):
            scores = dot(parts[at // sub][h], k_aug[h], NT)
            if edge_at is not None and at == (0 if edge_at == 0 else tile - sub):
                return jnp.where(edges[edge_at][:, :1] == row_ref[...], scores, masked_score)
            return jnp.concatenate(
                [
                    scores[:, :sub] + mask[:, :sub],
                    scores[:, sub : seq - sub],
                    scores[:, seq - sub :] + mask[:, seq - sub :],
                ],
                axis=1,
            )

        scores = scores_of(*chains[0])
        results = {}
        for n, (at, h) in enumerate(chains):
            if n + 1 < len(chains):
                later = scores_of(*chains[n + 1])
            peak = jnp.max(scores, axis=1, keepdims=True)
            numerators = jnp.exp2(scores - peak).astype(BF)
            if keep:
                e_ref[h, at : at + sub, :] = numerators
            total = dot(numerators, v_aug[h])
            where_sum = 64 if h == 0 else 0
            inverse = 1.0 / total[:, where_sum : where_sum + 1]
            results[h] = (total * inverse, inverse)
            if n + 1 < len(chains):
                scores = later
            if h == 1:
                done = jnp.where(low, results[0][0], results[1][0]).astype(BF)
                ctx_all[pair, pl.ds(start + at, sub), :] = done
                if keep:
                    ctx_ref[at : at + sub, :] = done
                    inv_ref[at : at + sub, :] = jnp.where(low, results[0][1], results[1][1])

    @pl.when(turned == 0)
    def _():
        body(0)

    @pl.when(turned == steps - 1)
    def _():
        body(1)

    @pl.when((turned > 0) & (turned < steps - 1))
    def _():
        body(None)

    owned = seq // groups
    owner = start // owned
    at = lax.rem(turned, owned // tile)
    source = ctx_all.at[pair, pl.ds(start, tile)]
    target = rows_ref.at[r, pair, pl.ds(pl.multiple_of(lax.rem(start, owned), tile), tile)]

    @pl.when(owner == r)
    def _():
        tiles.own(have, source, target, pair, at).start()

    @pl.when(owner != r)
    def _():
        tiles.copy(have, source, target, owner, pair, at).start()

    @pl.when((pair == pairs - 1) & (step == steps - 1))
    def _():
        tiles.finish(have, source, target)
        moves.last(sources, targets, scratch)


def own_rows_last(step, seq, tile, groups):
    s, r = place(groups)
    steps = seq // tile
    return lax.rem(step + (r + 1) * (steps // groups), steps)


def stream_row(docs_ref):
    return jnp.concatenate([docs_ref[i, 0:1, :] for i in range(docs_ref.shape[0])], axis=1)


def long_at(streams, groups, seq):
    shard = seq // (streams * groups)
    return streams * shard if groups > 1 else shard


def attention(x, weights, bias, docs, streams, groups, moves, moved, keep, collective_id, name):
    seq, depth = x.shape
    width = depth // groups
    pairs = width // 128
    tile = 512
    owned = seq // groups
    bag = Bag()
    bag.add("k_aug", pltpu.VMEM((2, seq, 128), BF))
    bag.add("v_aug", pltpu.VMEM((2, seq, 128), BF))
    bag.add("ctx_all", pltpu.VMEM((pairs, seq, 128), BF))
    bag.add("mask", pltpu.VMEM((1, seq), F32))
    bag.add("row", pltpu.VMEM((1, seq), F32))
    bag.add("edges", pltpu.VMEM((2, 256, 128), F32))
    tiles = Tiles(bag, "tiles", groups, pairs, owned // tile)
    for i, item in enumerate(moves.scratch()):
        bag.add(f"moves{i}", item)

    def constant(shape):
        return pl.BlockSpec(shape, lambda p, i: (0,) * len(shape))

    def turn(i):
        return own_rows_last(i, seq, tile, groups)

    part = pl.BlockSpec((tile, 128), lambda p, i: (turn(i), p))
    whole = pl.BlockSpec((seq, 128), lambda p, i: (0, p))
    any_space = pl.BlockSpec(memory_space=pl.ANY)
    wide = jax.ShapeDtypeStruct((seq, width), BF)
    outs = [whole, whole, any_space]
    shapes = [wide, wide, jax.ShapeDtypeStruct((groups, pairs, owned, 128), BF)]
    if keep:
        outs += [
            whole,
            pl.BlockSpec((2, tile, seq), lambda p, i: (p, turn(i), 0)),
            part,
            part,
            constant((seq, depth)),
        ]
        shapes += [
            wide,
            jax.ShapeDtypeStruct((2 * pairs, seq, seq), BF),
            wide,
            jax.ShapeDtypeStruct((seq, width), F32),
            jax.ShapeDtypeStruct((seq, depth), BF),
        ]
    return pl.pallas_call(
        functools.partial(forward_kernel, moves, keep, streams, groups, tile, bag, tiles),
        grid=(pairs, seq // tile),
        in_specs=[constant(a.shape) for a in (x, weights, bias, docs)]
        + moves.spaces(),
        out_specs=outs + moves.spaces(),
        out_shape=shapes + moves.out_shapes(),
        scratch_shapes=list(bag.items.values()),
        compiler_params=remote_params(collective_id),
        name=name,
    )(x, weights, bias, docs, *moved)


def split(matrix):
    upper = matrix.astype(BF)
    return upper, (matrix - upper.astype(F32)).astype(BF)


def backward_kernel(
    streams,
    groups,
    tile,
    bag,
    early,
    late,
    e_ref,
    q_ref,
    k_ref,
    v_ref,
    tq_ref,
    tk_ref,
    dc_ref,
    ctx_ref,
    inv_ref,
    docs_ref,
    small_ref,
    active_hbm,
    bin_hbm,
    d1_hbm,
    tokens_hbm,
    *rest,
):
    n_early = sum(job.count for job in early)
    sources, rest = rest[:n_early], rest[n_early:]
    grad_ref, *rest = rest
    early_out, rest = rest[:n_early], rest[n_early:]
    late_out, (gain_ref, bias_ref, shift_ref, *rest) = rest[: len(late)], rest[len(late) :]
    have = bag.bind(rest)
    at = 0
    for job in early:
        job.bind(sources[at : at + job.count], early_out[at : at + job.count], have)
        at += job.count
    for job, target in zip(late, late_out):
        job.bind(None, [target], have)

    pair, step = pl.program_id(0), pl.program_id(1)
    pairs, steps = len(late), q_ref.shape[0] // tile
    sub = min(256, tile)
    seq = k_ref.shape[0]
    share = 1.0 / seq
    time = pair * steps + step
    total_time = pairs * steps
    size = lax.axis_size("dp")
    here = lax.axis_index("dp")
    s, r = place(groups)
    rows, depth = d1_hbm.shape
    width = pairs * 128
    v_aug, dk_acc, dv_acc, grams = have["v_aug"], have["dk_acc"], have["dv_acc"], have["grams"]
    dq_all, d_act, active, weights = have["dq_all"], have["d_act"], have["active"], have["weights"]
    d_one, x_rows = have["d_one"], have["x_rows"]
    edges, in_big, pair_box = have["edges"], have["in_big"], have["pair_box"]
    row_ref = have["row"]
    along_z, cores, along_dp = stream_peers(streams, groups), core_peers(groups), dp_peers()

    def loads():
        sems = have["load"]
        return [
            pltpu.make_async_copy(active_hbm, active, sems.at[0]),
            pltpu.make_async_copy(bin_hbm, weights, sems.at[1]),
            pltpu.make_async_copy(d1_hbm, d_one, sems.at[2]),
            pltpu.make_async_copy(tokens_hbm.at[pl.ds(r * streams, streams)], x_rows, sems.at[3]),
        ]

    halves = tile // sub
    plan = []

    def at_time(when, work):
        plan.append((when, work))

    def due(half):
        for when, work in plan:
            if when % halves == half:
                pl.when(time == when // halves)(work)

    def begin():
        greet(along_z + cores + along_dp)
        for job in early:
            job.core_start()
        for copy in loads():
            copy.start()
        ids = stream_row(docs_ref)
        row_ref[...] = ids
        big_at = long_at(streams, groups, seq)
        big = ids[:, big_at : big_at + 1]
        for n, first in enumerate((0, seq - sub)):
            column = jnp.broadcast_to(ids[:, first : first + sub], (128, sub)).T
            edges[n] = column
            in_big[n] = jnp.where(column == big, 1.0, 0.0)

    def big_rows(ref):
        return jnp.concatenate(
            [
                (ref[:sub, :].astype(F32) * in_big[0]).astype(BF),
                ref[sub : seq - sub, :],
                (ref[seq - sub :, :].astype(F32) * in_big[1]).astype(BF),
            ],
            axis=0,
        )

    at_time(0, begin)
    unit = total_time * halves / 16
    left = []
    for n, job in enumerate(early):
        stages, times = job.stages(), EARLY_TIMES[n]
        if not job.two_step:
            times = times[:1] + times[2:5] + times[6:]
        for when, work in zip(times, stages):
            at_time(int(when * unit), work)
        left.append(stages[len(times) :])
    for p, job in enumerate(late[:-1]):
        first = (p + 1) * steps * halves
        for when, work in zip(LATE_TIMES, job.stages()):
            at_time(first + when, work)
        left.append(job.stages()[len(LATE_TIMES) :])

    def go_on(count):
        for unused in range(count):
            for queue in left:
                if queue:
                    queue.pop(0)()

    due(0)

    @pl.when(step == 0)
    def _():
        lane = lanes_of((seq, 128))
        low = lane < 64
        values = v_ref[...].astype(F32)
        v_aug[0] = jnp.where(low, values, jnp.where(lane < 66, 1.0, 0.0)).astype(BF)
        v_aug[1] = jnp.where(low, jnp.where(lane < 2, 1.0, 0.0), values).astype(BF)
        dk_acc[...] = jnp.zeros_like(dk_acc)
        dv_acc[...] = jnp.zeros_like(dv_acc)
        kb, tkb, qb, tqb = (big_rows(ref) for ref in (k_ref, tk_ref, q_ref, tq_ref))
        same_head = (lax.broadcasted_iota(jnp.int32, (128, 128), 0) < 64) == (
            lanes_of((128, 128)) < 64
        )
        for i, (a, b) in enumerate(((kb, kb), (tkb, kb), (qb, qb), (tqb, qb))):
            gram = jnp.where(same_head, dot(a, b, TN) * share, 0.0)
            grams[2 * i], grams[2 * i + 1] = split(gram)

    start = pl.multiple_of(step * tile, tile)
    low = lanes_of((sub, 128)) < 64
    lane = lanes_of((sub, 128))

    def prepare(at):
        here_rows = pl.ds(start + at, sub)
        q8, tq8 = q_ref[here_rows, :], tq_ref[here_rows, :]
        scaled = dc_ref[at : at + sub, :].astype(F32) * inv_ref[at : at + sub, :]
        product = scaled * ctx_ref[at : at + sub, :].astype(F32)
        augmented = []
        for h in range(2):
            mine = low if h == 0 else jnp.logical_not(low)
            delta = -jnp.sum(jnp.where(mine, product, 0.0), axis=1, keepdims=True)
            upper = delta.astype(BF).astype(F32)
            first = 64 if h == 0 else 0
            extra = jnp.where(
                lane == first, upper, jnp.where(lane == first + 1, delta - upper, 0.0)
            )
            augmented.append(jnp.where(mine, scaled, extra).astype(BF))
        q_turned = q8.astype(F32).T.astype(BF)
        dc_turned = scaled.T.astype(BF)
        return here_rows, q8, tq8, augmented, q_turned, dc_turned

    def body(edge, half):
        ready = {half * sub: prepare(half * sub)}
        chains = [(half * sub, h) for h in range(2)]
        edge_at = {None: None, 0: 0, 1: tile - sub}[edge]
        columns = slice(0, sub) if edge == 0 else slice(seq - sub, seq)

        def d_probs_of(at, h):
            return dot(ready[at][3][h], v_aug[h], NT)

        d_probs = d_probs_of(*chains[0])
        d_queries = {}
        for n, (at, h) in enumerate(chains):
            if n + 1 < len(chains):
                later = d_probs_of(*chains[n + 1])
            here_rows, q8, tq8, unused, q_turned, dc_turned = ready[at]
            mine = low if h == 0 else jnp.logical_not(low)
            numerators = e_ref[h, at : at + sub, :]
            d_scores = numerators.astype(F32) * d_probs
            if edge is not None and at == edge_at:
                q_mine = jnp.where(mine, q8, 0.0).astype(BF)
                tq_mine = jnp.where(mine, tq8, 0.0).astype(BF)
                gap = dot(q_mine, k_ref[columns, :], NT) - dot(tq_mine, tk_ref[columns, :], NT)
                same = jnp.where(edges[edge][:, :1] == row_ref[:, columns], share, 0.0)
                gap = gap * (same * (1.0 - in_big[edge][:, :1]))
                if edge == 0:
                    d_scores = jnp.concatenate(
                        [d_scores[:, :sub] + gap, d_scores[:, sub:]], axis=1
                    )
                else:
                    d_scores = jnp.concatenate(
                        [d_scores[:, : seq - sub], d_scores[:, seq - sub :] + gap], axis=1
                    )
            d_scores = d_scores.astype(BF)
            mine = slice(64 * h, 64 * h + 64)
            dv_acc[mine, :] += dot(dc_turned[mine, :], numerators)
            d_queries[h] = dot(d_scores, k_ref[...])
            dk_acc[mine, :] += dot(q_turned[mine, :], d_scores)
            if h == 1:
                d_query = jnp.where(low, d_queries[0], d_queries[1])
                qb, tqb = q8, tq8
                if edge is not None and at == edge_at:
                    qb = (q8.astype(F32) * in_big[edge]).astype(BF)
                    tqb = (tq8.astype(F32) * in_big[edge]).astype(BF)
                d_query += dot(qb, grams[0]) + dot(qb, grams[1])
                d_query -= dot(tqb, grams[2]) + dot(tqb, grams[3])
                dq_all[here_rows, :] = (d_query * 0.125).astype(BF)
            if n + 1 < len(chains):
                d_probs = later

    for half in range(halves):
        if half:
            due(half)
        edge, at_edge = None, None
        if half == 0:
            edge, at_edge = 0, step == 0
        elif half == halves - 1:
            edge, at_edge = 1, step == steps - 1
        if edge is not None:
            pl.when(at_edge)(functools.partial(body, edge, half))
            pl.when(jnp.logical_not(at_edge))(functools.partial(body, None, half))
        else:
            body(None, half)

    def pair_end(p):
        job = late[p]
        kb, tkb = big_rows(k_ref), big_rows(tk_ref)
        d_key = dk_acc[...].T
        d_key += dot(kb, grams[4]) + dot(kb, grams[5]) - dot(tkb, grams[6]) - dot(tkb, grams[7])
        d_value = dv_acc[...].T.astype(BF)
        d_query = dq_all[...]
        d_pair = jnp.concatenate([d_query, d_key.astype(BF), d_value], axis=1)
        if p == 0:
            for copy in loads():
                copy.wait()
        columns = slice(p * 128, (p + 1) * 128)
        bins = jnp.concatenate([weights[0, i, :, columns] for i in range(3)], axis=1)
        chunk = depth // size
        half = job.get("half", 0)
        partial = dot(active[...], d_pair, TN).astype(job.wires[0])
        for d in range(size):
            half[d] = partial[d * chunk : (d + 1) * chunk, :]
        if p == pairs - 1:
            job.dp_start()
        if p < pairs - 1:
            if p == 0:
                d_act[...] = dot(d_pair, bins, NT)
            else:
                d_act[...] += dot(d_pair, bins, NT)
        else:
            pair_box[...] = d_pair
            for j in range(1, groups + 1):
                at = pl.ds(pl.multiple_of(lax.rem(r + j, groups) * rows, rows), rows)
                total = dot(pair_box[at, :], bins, NT)
                if p > 0:
                    total = total + d_act[at, :]
                if j < groups:
                    have["outbox"][j - 1] = total.astype(BF)
                    core_copies()[j - 1].start()
                else:
                    d_act[at, :] = total
        sums = have["sums"]
        sums[0:1, columns] = jnp.sum(d_query.astype(F32), axis=0, keepdims=True)
        sums[1:2, columns] = jnp.sum(d_value.astype(F32), axis=0, keepdims=True)

    def core_copies():
        return [
            remote(
                have["outbox"].at[j - 1],
                have["inbox"].at[j - 1],
                have["core_s"].at[j],
                have["core_r"].at[j],
                cores[j - 1],
            )
            for j in range(1, groups)
        ]

    def small_copies(stage, peers, base):
        return [
            remote(
                have["small"].at[stage],
                have["small_box"].at[base + d],
                have["small_s"].at[base + d],
                have["small_r"].at[base + d],
                peer,
            )
            for d, peer in enumerate(peers)
        ]

    def small_start(stage, peers, base):
        for copy in small_copies(stage, peers, base):
            copy.start()

    def small_sum(stage, peers, base):
        for copy in small_copies(stage, peers, base):
            copy.wait_recv()
        total = have["small"][stage]
        for d in range(len(peers)):
            total = total + have["small_box"][base + d]
        return total

    for p in range(pairs - 1):

        @pl.when((pair == p) & (step == steps - 1))
        def _():
            pair_end(p)

    @pl.when(time == total_time - 1)
    def _():
        pair_end(pairs - 1)
        last = late[-1]
        small = have["small"]
        small[0] = small_ref[...]
        for i in range(2):
            vector = have["sums"][i : i + 1, :]
            small[0, 2 + i : 3 + i, :] = jnp.concatenate(
                [jnp.where(r == j, vector, 0.0) for j in range(groups)], axis=1
            )
        small_start(0, along_dp, 0)
        go_on(TAIL[0])
        last.z_start()
        last.z_back()
        for copy in core_copies():
            copy.wait_recv()
        shard = rows // streams
        back_copies = []
        blocks = have["blocks"]
        order = [2, 1, 3] if streams == 4 else list(range(1, streams))
        for d in order + [0]:
            target = lax.rem(s + d, streams)
            here_rows = pl.ds(pl.multiple_of(target * shard, shard), shard)
            bent = jnp.tanh(x_rows[target].astype(F32) * (1.0 / clip_level))
            total = d_act[pl.ds(pl.multiple_of(r * rows + target * shard, shard), shard), :]
            for j in range(groups - 1):
                total = total + have["inbox"][j, here_rows, :].astype(F32)
            blocks[target] = (d_one[here_rows, :] + total * (1.0 - bent * bent)).astype(BF)
            if d:
                copy = remote(
                    blocks.at[target],
                    grad_ref.at[s],
                    have["grad_s"].at[d],
                    have["grad_r"].at[d],
                    along_z[d - 1],
                )
            else:
                copy = pltpu.make_async_copy(blocks.at[s], grad_ref.at[s], have["grad_s"].at[0])
            copy.start()
            back_copies.append(copy)
        small[1] = small_sum(0, along_dp, 0)
        small_start(1, along_z, size)
        go_on(TAIL[1])
        small[2] = small_sum(1, along_z, size)
        small_start(2, cores, size + streams)
        go_on(TAIL[2])
        last.dp_back()
        summed = small_sum(2, cores, size + streams)
        gain_ref[...] = summed[0:2, :]
        bias_ref[...] = summed[2:8, :]
        for i in range(shift_ref.shape[1] // depth):
            shift_ref[:, i * depth : (i + 1) * depth] = summed[8 + i : 9 + i, :]
        go_on(TAIL[3])
        last.core_back()
        go_on(8)
        for copy in back_copies:
            copy.wait()
        for job in early + late:
            job.end()
        for copy in (
            core_copies()
            + small_copies(0, along_dp, 0)
            + small_copies(1, along_z, size)
            + small_copies(2, cores, size + streams)
        ):
            copy.wait_send()


TWO_STEP = False
TAIL = (1, 1, 0, 0)
EARLY_TIMES = ((2, 0, 7, 9, 12), (4, 0, 12, 14))
LATE_TIMES = (0, 5, 7)


def attention_back(
    streams,
    groups,
    numerators,
    queries,
    keys,
    values,
    teacher_queries,
    teacher_keys,
    d_context,
    context,
    inverse,
    docs,
    small,
    active,
    bin_own,
    d_one,
    tokens,
    early_arrays,
    up_width,
    collective_id,
):
    seq, width = queries.shape
    pairs = width // 128
    tile = 512
    rows, depth = d_one.shape
    size = lax.axis_size("dp")
    shard = rows // streams
    bag = Bag()
    bag.add("v_aug", pltpu.VMEM((2, seq, 128), BF))
    bag.add("dk_acc", pltpu.VMEM((128, seq), F32))
    bag.add("dv_acc", pltpu.VMEM((128, seq), F32))
    bag.add("grams", pltpu.VMEM((8, 128, 128), BF))
    bag.add("dq_all", pltpu.VMEM((seq, 128), BF))
    bag.add("d_act", pltpu.VMEM((seq, depth), F32))
    bag.add("active", pltpu.VMEM((seq, depth), BF))
    bag.add("weights", pltpu.VMEM((1, 3, depth, width), BF))
    bag.add("d_one", pltpu.VMEM((rows, depth), F32))
    bag.add("x_rows", pltpu.VMEM((streams, shard, depth), BF))
    bag.add("load", dma(4))
    bag.add("sums", pltpu.VMEM((8, width), F32))
    bag.add("outbox", pltpu.VMEM((groups - 1, rows, depth), BF))
    bag.add("inbox", pltpu.VMEM((groups - 1, rows, depth), BF))
    bag.add("core_s", dma(groups))
    bag.add("core_r", dma(groups))
    bag.add("blocks", pltpu.VMEM((streams, shard, depth), BF))
    bag.add("grad_s", dma(streams))
    bag.add("grad_r", dma(streams))
    count = size + streams + groups
    bag.add("small", pltpu.VMEM((3,) + small.shape, F32))
    bag.add("small_box", pltpu.VMEM((count,) + small.shape, F32))
    bag.add("small_s", dma(count))
    bag.add("small_r", dma(count))
    bag.add("row", pltpu.VMEM((1, seq), F32))
    bag.add("pair_box", pltpu.VMEM((seq, 3 * 128), BF))
    bag.add("edges", pltpu.VMEM((2, 256, 128), F32))
    bag.add("in_big", pltpu.VMEM((2, 256, 128), F32))
    early, flat = [], []
    for n, arrays in enumerate(early_arrays):
        job = Reduce(bag, f"early{n}", streams, groups, [a.shape for a in arrays], True, TWO_STEP)
        early.append(job)
        flat += [
            a.reshape(groups, size, chunk, cols) for a, (chunk, cols) in zip(arrays, job.shapes)
        ]
    late = [
        Reduce(bag, f"late{p}", streams, groups, [(depth, 3 * 128)], False, False)
        for p in range(pairs)
    ]
    part = pl.BlockSpec((tile, 128), lambda p, i: (i, p))
    any_space = pl.BlockSpec(memory_space=pl.ANY)

    whole = pl.BlockSpec((seq, 128), lambda p, i: (0, p))

    def constant(shape):
        return pl.BlockSpec(shape, lambda p, i: (0,) * len(shape))

    small_shapes = [(2, depth), (6, depth), (1, up_width)]
    early_shapes = [shape for job in early for shape in job.out_shapes()]
    late_shapes = [shape for job in late for shape in job.out_shapes()]
    results = pl.pallas_call(
        functools.partial(backward_kernel, streams, groups, tile, bag, early, late),
        grid=(pairs, seq // tile),
        in_specs=[
            pl.BlockSpec((2, tile, seq), lambda p, i: (p, i, 0)),
            whole,
            whole,
            whole,
            whole,
            whole,
            part,
            part,
            part,
            constant(docs.shape),
            constant(small.shape),
        ]
        + [any_space] * (4 + len(flat)),
        out_specs=[any_space] * (1 + len(early_shapes) + len(late_shapes))
        + [constant(shape) for shape in small_shapes],
        out_shape=[jax.ShapeDtypeStruct((streams, shard, depth), BF)]
        + early_shapes
        + late_shapes
        + [jax.ShapeDtypeStruct(shape, F32) for shape in small_shapes],
        scratch_shapes=list(bag.items.values()),
        compiler_params=remote_params(collective_id),
        name="attention_back",
    )(
        numerators,
        queries,
        keys,
        values,
        teacher_queries,
        teacher_keys,
        d_context,
        context,
        inverse,
        docs,
        small,
        active,
        bin_own,
        d_one,
        tokens,
        *flat,
    )
    grad_tokens, *rest = results
    early_sums = rest[: len(flat)]
    late_sums = rest[len(flat) : -3]
    shapes = [a.shape for arrays in early_arrays for a in arrays]
    return (
        grad_tokens,
        [e.reshape(shape) for e, shape in zip(early_sums, shapes)],
        [l.reshape(groups, depth, 3 * 128) for l in late_sums],
        list(rest[-3:]),
    )


def middle_kernel(
    streams,
    groups,
    bag,
    tiles,
    x_ref,
    tx_ref,
    cot_ref,
    ctx_ref,
    tctx_ref,
    bo_hbm,
    bup_hbm,
    bdown_hbm,
    to_hbm,
    tup_hbm,
    tdown_hbm,
    sg_ref,
    sb_ref,
    sub_ref,
    tg_ref,
    tb_ref,
    tub_ref,
    out_ref,
    d1_ref,
    dctx_ref,
    gout_ref,
    gup_ref,
    gdown_ref,
    small_ref,
    *rest,
):
    have = bag.bind(rest)
    gout_acc, gup_acc, gdown_acc = have["gout"], have["gup"], have["gdown"]
    out_box, d_box = have["out_box"], have["d_box"]
    step = pl.program_id(0)
    far = (to_hbm, bo_hbm, tup_hbm, bup_hbm, tdown_hbm, bdown_hbm)
    to_ref, bo_ref, tup_ref, bup_ref, tdown_ref, bdown_ref = near = [
        have[f"weight{i}"] for i in range(6)
    ]
    loads = [
        pltpu.make_async_copy(source, target, have["weight_sems"].at[i])
        for i, (source, target) in enumerate(zip(far, near))
    ]

    def ready(which):
        @pl.when(step == 0)
        def _():
            for i in which:
                loads[i].wait()

    steps = pl.num_programs(0)
    width = ctx_ref.shape[1] * 128
    tile, depth = cot_ref.shape
    n_steps = out_box.shape[0]
    shard = n_steps * tile // streams
    s, r = place(groups)
    along_z = stream_peers(streams, groups)
    turned = row_tile(step, n_steps, streams, groups)
    start = pl.multiple_of(turned * tile, tile)

    @pl.when(step == 0)
    def _():
        for copy in loads:
            copy.start()
        greet(along_z + core_peers(groups))

    @pl.when(step == 0)
    def _():
        for ref in (gout_acc, gup_acc, gdown_acc, small_ref):
            ref[...] = jnp.zeros_like(ref)

    def row(ref, i):
        return ref[i : i + 1, :]

    pieces = [(j, p) for j in range(groups) for p in range(ctx_ref.shape[1])]
    ff = bup_ref.shape[1]
    wide = min(512, ff)
    chunks = [slice(i, i + wide) for i in range(0, ff, wide)]

    ready((0, 1))
    tctx = jnp.concatenate([tctx_ref[j, p] for j, p in pieces], axis=1)
    t_att = dot(tctx, to_ref[...]) + row(tb_ref, 2)
    context = jnp.concatenate([ctx_ref[j, p] for j, p in pieces], axis=1).astype(F32)
    bent = jnp.tanh(context * (1.0 / clip_level))
    ctx_active = (clip_level * bent).astype(BF)
    ctx_slope = 1.0 - bent * bent
    attended = dot(ctx_active, bo_ref[...]) + row(sb_ref, 2)
    t_hidden = layer_norm(tx_ref[...].astype(F32) + t_att, row(tg_ref, 0), row(tb_ref, 3))[0]
    hidden, normed_one, inverse_one = layer_norm(
        x_ref[...].astype(F32) + attended, row(sg_ref, 0), row(sb_ref, 3)
    )
    bent = jnp.tanh(hidden * (1.0 / clip_level))
    hidden_active = (clip_level * bent).astype(BF)
    hidden_slope = 1.0 - bent * bent
    t_low = t_hidden.astype(BF)

    def up(i):
        return dot(t_low, tup_ref[:, chunks[i]]), dot(hidden_active, bup_ref[:, chunks[i]])

    ready((2, 3, 4, 5))
    ahead = up(0)
    t_branch, branch, actives, slopes = None, None, [], []
    for i, at in enumerate(chunks):
        t_pre, inner_pre = ahead
        if i + 1 < len(chunks):
            ahead = up(i + 1)
        t_inner = gelu_parts(t_pre + tub_ref[:, at])[0]
        inner_pre = inner_pre + sub_ref[:, at]
        inner_act, phi = gelu_parts(inner_pre)
        bent = jnp.tanh(inner_act * (1.0 / clip_level))
        inner_active = (clip_level * bent).astype(BF)
        t_term = dot(t_inner.astype(BF), tdown_ref[at, :])
        term = dot(inner_active, bdown_ref[at, :])
        t_branch = t_term if i == 0 else t_branch + t_term
        branch = term if i == 0 else branch + term
        actives.append(inner_active)
        slopes.append(
            (1.0 - bent * bent)
            * (phi + inner_pre * jnp.exp(-0.5 * inner_pre * inner_pre) * 0.3989422804014327)
        )
    t_out = layer_norm(t_hidden + t_branch + row(tb_ref, 4), row(tg_ref, 1), row(tb_ref, 5))[0]
    branch = branch + row(sb_ref, 4)
    output, normed_two, inverse_two = layer_norm(hidden + branch, row(sg_ref, 1), row(sb_ref, 5))
    out_box[step] = output.astype(BF)
    per_tile = tile // shard
    for n in range(per_tile):
        block = turned * per_tile + n
        source = out_box.at[step, pl.ds(n * shard, shard)]

        @pl.when(block == s)
        def _():
            pltpu.make_async_copy(source, out_ref.at[s], have["out_s"].at[s]).start()

        @pl.when(block != s)
        def _():
            remote(
                source,
                out_ref.at[s],
                have["out_s"].at[block],
                have["out_r"].at[s],
                {"blk": block * groups + r},
            ).start()
    upstream = cot_ref[...].astype(F32) + 0.5 * (output - t_out)
    d_two = norm_back(upstream, row(sg_ref, 1), normed_two, inverse_two)
    d_branch = d_two.astype(BF)

    def down(i):
        return dot(d_branch, bdown_ref[chunks[i], :], NT)

    ahead = down(0)
    through = None
    for i, at in enumerate(chunks):
        d_inner = ahead
        if i + 1 < len(chunks):
            ahead = down(i + 1)
        d_inner = (d_inner * slopes[i]).astype(BF)
        gdown_acc[at, :] += dot(actives[i], d_branch, TN)
        gup_acc[:, at] += dot(hidden_active, d_inner, TN)
        term = dot(d_inner, bup_ref[:, at], NT)
        through = term if i == 0 else through + term
        d_shift = jnp.sum(d_inner.astype(F32), axis=0, keepdims=True)
        for n in range(wide // depth):
            line = 8 + (i * wide) // depth + n
            small_ref[line : line + 1, :] += d_shift[:, n * depth : (n + 1) * depth]
    d_hidden = d_two + through * hidden_slope
    d_one = norm_back(d_hidden, row(sg_ref, 0), normed_one, inverse_one)
    d1_ref[...] = d_one
    d_attended = d_one.astype(BF)
    gout_acc[...] += dot(ctx_active, d_attended, TN)
    d_context = (dot(d_attended, bo_ref[...], NT) * ctx_slope).astype(BF)
    place_rows = pl.ds(pl.multiple_of(r * n_steps * tile + start, tile), tile)
    for j in range(groups):
        d_box[step, j] = d_context[:, j * width : (j + 1) * width]
        piece, target = d_box.at[step, j], dctx_ref.at[place_rows]

        @pl.when(r == j)
        def _():
            tiles.own(have, piece, target, 0, step).start()

        @pl.when(r != j)
        def _():
            tiles.copy(have, piece, target, j, 0, step).start()


    def total(value):
        return jnp.sum(value, axis=0, keepdims=True)

    sums = [
        (0, d_hidden * normed_one),
        (1, upstream * normed_two),
        (4, d_attended.astype(F32)),
        (5, d_hidden),
        (6, d_branch.astype(F32)),
        (7, upstream),
    ]
    for i, value in sums:
        small_ref[i : i + 1, :] += total(value)
    @pl.when(step == steps - 1)
    def _():
        tiles.finish(have, d_box.at[0, 0], dctx_ref.at[place_rows])
        source = out_box.at[0, pl.ds(0, shard)]
        pltpu.make_async_copy(source, out_ref.at[s], have["out_s"].at[s]).wait()
        for d, peer in enumerate(along_z, 1):
            block = lax.rem(s + d, streams)
            remote(
                source, out_ref.at[block], have["out_s"].at[block], have["out_r"].at[block], peer
            ).wait()
        gout_ref[...] = gout_acc[...].astype(BF)
        gup_ref[...] = gup_acc[...].astype(BF)
        gdown_ref[...] = gdown_acc[...].astype(BF)


def row_tile(step, steps, streams, groups):
    s, r = place(groups)
    return lax.rem(s // (streams // steps) + 1 + step, steps)


def middle(streams, groups, x, tx, cot, ctx, tctx, weights, teacher_weights, vectors, collective_id):
    rows, depth = cot.shape
    ff = weights[1].shape[1]
    tile = min(256, rows)
    pairs = ctx.shape[1]
    width = pairs * 128
    steps = rows // tile
    shard = rows // streams

    def turn(i):
        return row_tile(i, steps, streams, groups)

    def stream_tile(i):
        return lax.rem(lax.axis_index("blk"), groups) * steps + turn(i)

    tall = pl.BlockSpec((tile, depth), lambda i: (turn(i), 0))
    of_stream = pl.BlockSpec((tile, depth), lambda i: (stream_tile(i), 0))
    split_rows = pl.BlockSpec((groups, pairs, tile, 128), lambda i: (0, 0, turn(i), 0))
    any_space = pl.BlockSpec(memory_space=pl.ANY)

    def full(shape):
        return pl.BlockSpec(shape, lambda i: (0,) * len(shape))

    out_full = [(depth, depth), (depth, ff), (ff, depth), (16, depth)]
    bag = Bag()
    for name, shape in zip(("gout", "gup", "gdown"), out_full):
        bag.add(name, pltpu.VMEM(shape, F32))
    for i in range(3):
        bag.add(f"weight{2 * i}", pltpu.VMEM(teacher_weights[i].shape, BF))
        bag.add(f"weight{2 * i + 1}", pltpu.VMEM(weights[i].shape, BF))
    bag.add("weight_sems", dma(6))
    bag.add("out_box", pltpu.VMEM((steps, tile, depth), BF))
    bag.add("d_box", pltpu.VMEM((steps, groups, tile, width), BF))
    bag.add("out_s", dma(streams))
    bag.add("out_r", dma(streams))
    tiles = Tiles(bag, "tiles", groups, 1, steps)
    return pl.pallas_call(
        functools.partial(middle_kernel, streams, groups, bag, tiles),
        grid=(steps,),
        in_specs=[of_stream, of_stream, tall, split_rows, split_rows]
        + [any_space] * 6
        + [full(a.shape) for a in vectors],
        out_specs=[any_space, tall, any_space] + [full(s) for s in out_full],
        out_shape=[
            jax.ShapeDtypeStruct((streams, shard, depth), BF),
            jax.ShapeDtypeStruct((rows, depth), F32),
            jax.ShapeDtypeStruct((rows * groups, width), BF),
        ]
        + [jax.ShapeDtypeStruct(s, BF if i < 3 else F32) for i, s in enumerate(out_full)],
        scratch_shapes=list(bag.items.values()),
        compiler_params=remote_params(collective_id),
        name="middle",
    )(x, tx, cot, ctx, tctx, *weights, *teacher_weights, *vectors)


def latent_columns(latent, grad, out):
    rows = latent.shape[0]
    size = min(256, rows)
    chunks = [slice(i, i + size) for i in range(0, rows, size)]
    squares = jnp.zeros((1, latent.shape[1]), F32)
    for at in chunks:
        matrix = latent[at, :].astype(F32)
        squares = squares + jnp.sum(matrix * matrix, axis=0, keepdims=True)
    scale = jnp.sqrt(squares * (1.0 / rows) + 1e-06)
    twice = 2.0 / scale
    through_scale = jnp.zeros_like(squares)
    for at in chunks:
        matrix, upstream = latent[at, :].astype(F32), grad[at, :].astype(F32)
        inner = matrix * twice
        bent = jnp.tanh(inner)
        slope = 1.0 - bent * bent
        through_scale = through_scale + jnp.sum(
            upstream * (bent - inner * slope), axis=0, keepdims=True
        )
        out[at, :] = upstream * (2.0 * slope)
    factor = through_scale / (rows * scale)
    for at in chunks:
        out[at, :] = out[at, :] + latent[at, :].astype(F32) * factor


def latent_grads_kernel(pairs, passed, lq, lo, lu, ld, *refs):
    late, (go, gu, gd, *refs) = refs[:pairs], refs[pairs:]
    come, (oq, oo, ou, od, *gone) = refs[:passed], refs[passed:]
    for source, target in zip(come, gone):
        target[...] = source[...]
    for p in range(pairs):

        @pl.when(lax.rem(pl.program_id(0), pairs) == p)
        def _():
            for i in range(3):
                latent_columns(lq.at[i], late[p].at[0, :, i * 128 : (i + 1) * 128], oq.at[i])

    latent_columns(lo, go, oo)
    latent_columns(ld, gd, od)
    for i in range(0, lu.shape[1], 128):
        at = slice(i, i + 128)
        latent_columns(lu.at[:, at], gu.at[:, at], ou.at[:, at])


def latent_grads(latents, late, early, tall, small):
    pairs = len(late)
    groups, depth, wide = late[0].shape
    steps = groups * pairs
    qkv = pl.BlockSpec((3, depth, depth // steps), lambda i: (0, 0, i))
    flat = [pl.BlockSpec((a.shape[0], a.shape[1] // steps), lambda i: (0, i)) for a in latents[1:]]
    handed = [
        pl.BlockSpec((a.shape[0] // steps,) + a.shape[1:], lambda i: (i, 0, 0)) for a in tall
    ] + [pl.BlockSpec(a.shape, lambda i: (0, 0)) for a in small]
    return pl.pallas_call(
        functools.partial(latent_grads_kernel, pairs, len(handed)),
        grid=(steps,),
        in_specs=[qkv]
        + flat
        + [pl.BlockSpec((1, depth, wide), lambda i: (i // pairs, 0, 0))] * pairs
        + flat
        + handed,
        out_specs=[qkv] + flat + handed,
        out_shape=[jax.ShapeDtypeStruct(a.shape, F32) for a in latents]
        + [jax.ShapeDtypeStruct(a.shape, a.dtype) for a in tall + small],
        compiler_params=pltpu.CompilerParams(vmem_limit_bytes=VMEM_BYTES),
        name="latent_grads",
    )(*latents, *late, *early, *tall, *small)


def shards(
    tokens,
    teacher_tokens,
    segment_ids,
    cotangent,
    latent_qkv,
    latent_out,
    latent_up,
    latent_down,
    student_gain,
    student_bias,
    student_up_bias,
    teacher_qkv,
    teacher_out,
    teacher_up,
    teacher_down,
    teacher_gain,
    teacher_bias,
    teacher_up_bias,
):
    streams, shard_len, depth = tokens.shape
    blocks = lax.axis_size("blk")
    groups = blocks // streams
    seq = shard_len * blocks
    rows = seq // groups
    block = (shard_len, depth)
    gather, swap = Gather(streams, groups, block, BF), Swap(streams, groups, block, BF)
    bin_own, bin_out, bin_up, bin_down, token_blocks, qkv_parts, docs = intake(
        Moves(
            gather,
            Spread(teacher_qkv.shape, BF),
            Gather(streams, groups, (8, shard_len), F32),
        ),
        groups,
        [latent_qkv, latent_out, latent_up, latent_down],
        segment_ids,
        [tokens, teacher_qkv],
        1,
    )
    stream_tokens = token_blocks.reshape(seq, depth)
    (
        queries,
        keys,
        ctx_rows,
        values,
        numerators,
        context,
        inverse,
        active,
        teacher_blocks,
        up_parts,
        out_parts,
    ) = attention(
        stream_tokens,
        bin_own,
        student_bias,
        docs,
        streams,
        groups,
        Moves(gather, Spread(teacher_up.shape, BF), Spread(teacher_out.shape, BF)),
        [teacher_tokens, teacher_up, teacher_out],
        True,
        2,
        "attention_student",
    )
    teacher_stream = teacher_blocks.reshape(seq, depth)
    teacher_queries, teacher_keys, tctx_rows, cot_blocks, down_parts = attention(
        teacher_stream,
        qkv_parts,
        teacher_bias,
        docs,
        streams,
        groups,
        Moves(swap, Spread(teacher_down.shape, BF), others=[gather]),
        [cotangent, teacher_down],
        False,
        3,
        "attention_teacher",
    )
    output, d_one, d_context, g_out, g_up, g_down, small = middle(
        streams,
        groups,
        stream_tokens,
        teacher_stream,
        cot_blocks.reshape(rows, depth),
        ctx_rows,
        tctx_rows,
        [bin_out, bin_up, bin_down],
        [
            out_parts.reshape(-1, depth),
            up_parts.reshape(depth, -1),
            down_parts.reshape(-1, depth),
        ],
        [
            student_gain,
            student_bias,
            student_up_bias.reshape(1, -1),
            teacher_gain,
            teacher_bias,
            teacher_up_bias.reshape(1, -1),
        ],
        4,
    )
    grads = [[g_up], [g_down, g_out]]
    in_kernel = depth % (16 * blocks * lax.axis_size("dp")) == 0
    grad_tokens, early, late, small = attention_back(
        streams,
        groups,
        numerators,
        queries,
        keys,
        values,
        teacher_queries,
        teacher_keys,
        d_context,
        context,
        inverse,
        docs,
        small,
        active,
        bin_own,
        d_one,
        token_blocks,
        grads if in_kernel else [],
        latent_up.shape[1],
        6,
    )
    if not in_kernel:
        early = lax.psum((g_up, g_down, g_out), ("dp", "blk"))
    grad_qkv, grad_out, grad_up, grad_down, output, grad_tokens, gain, bias, shift = latent_grads(
        [latent_qkv, latent_out, latent_up, latent_down],
        late,
        [early[2], early[0], early[1]],
        [output, grad_tokens],
        small,
    )
    return (
        output,
        grad_tokens,
        grad_qkv,
        grad_out,
        grad_up,
        grad_down,
        gain,
        bias,
        shift.reshape(-1),
    )


def solution(mesh):
    return jax.shard_map(
        shards,
        mesh=mesh,
        in_specs=(
            P("dp", "blk", None),
            P("dp", "blk", None),
            P("dp", "blk"),
            P("dp", "blk", None),
            P(),
            P(),
            P(),
            P(),
            P(),
            P(),
            P(),
            P(None, "dp", None),
            P("dp", None),
            P("dp", None),
            P("dp", None),
            P(),
            P(),
            P(),
        ),
        out_specs=(P("dp", "blk", None), P("dp", "blk", None), P(), P(), P(), P(), P(), P(), P()),
        check_vma=False,
    )
```

profile of v0, /device:TPU:0, one launch (start us, length us, event | category | flops | bytes accessed | tf_op | source)
XLA Modules:
  0.0 268.1 jit_solution(2797524085800891468)
XLA Ops:
  0.6 33.2 %intake.1 = (bf16[1,3,512,256]{3,2,1,0:T(8,128)(2,1)}, bf16[512,512]{1,0:T(8,128)(2,1)}, bf16[512,2048]{1,0:T(8,128)(2,1)}, bf16[2048,512]{1,0:T(8,128)(2,1)}, b...) custom-call(bf16[3,512,512]{2,1,0:T(8,128)(2,1)} %lq.1, bf16[512,512]{1,0:T(8,128)(2,1)} %lo.1, ...), custom_call_target="tpu_custom_call" | custom-call | tf_op jit(solution)/shard_map/intake/pallas_call | solution.py:639
  33.8 41.2 %attention_student.1 = (bf16[2048,256]{1,0:T(8,128)(2,1)}, bf16[2048,256]{1,0:T(8,128)(2,1)}, bf16[2,2,1024,128]{3,2,1,0:T(8,128)(2,1)}, bf16[2048,256]{1,0:T(8,...) custom-call(bf16[2048,512]{1,0:T(8,128)(2,1)} %bitcast.17, ...), custom_call_target="tpu_custom_call" | custom-call | tf_op jit(solution)/shard_map/attention_student/pallas_call | solution.py:880
  75.0 36.9 %attention_teacher.1 = (bf16[2048,256]{1,0:T(8,128)(2,1)}, bf16[2048,256]{1,0:T(8,128)(2,1)}, bf16[2,2,1024,128]{3,2,1,0:T(8,128)(2,1)}, bf16[4,256,512]{2,1,0:T(8,128)(2,1)}, bf16[4,512,512]{2,1,0:T(8,128)(2,1)}) custom-call(bf16[2048,512]{1,0:T(8,128)(2,1)} %bitcast.19, bf16[4,3,128,512]{3,2,1,0:T(8,128)(2,1)} %get-tuple-element.65.w_ref, ...), custom_call_target="tpu_custom_call" | custom-call | tf_op jit(solution)/shard_map/attention_teacher/pallas_call | solution.py:880
  112.0 37.9 %middle.1 = (bf16[4,256,512]{2,1,0:T(8,128)(2,1)}, f32[1024,512]{1,0:T(8,128)}, bf16[2048,256]{1,0:T(8,128)(2,1)}, bf16[512,512]{1,0:T(8,128)(2,1)}, bf16[512,20...) custom-call(bf16[2048,512]{1,0:T(8,128)(2,1)} %bitcast.18, bf16[2048,512]{1,0:T(8,128)(2,1)} %bitcast.20, ...), custom_call_target="tpu_custom_call" | custom-call | tf_op jit(solution)/shard_map/middle/pallas_call | solution.py:1672
  149.8 103.9 %attention_back.1 = (bf16[4,256,512]{2,1,0:T(8,128)(2,1)}, bf16[2,4,4,16,2048]{4,3,2,1,0:T(8,128)(2,1)}, bf16[2,4,4,64,512]{4,3,2,1,0:T(8,128)(2,1)}, bf16[2,4,4...) custom-call(bf16[4,2048,2048]{2,1,0:T(8,128)(2,1)} %get-tuple-elemen, ...), custom_call_target="tpu_custom_call" | custom-call | tf_op jit(solution)/shard_map/attention_back/pallas_call | solution.py:1363
  253.7 14.1 %latent_grads.1 = (f32[3,512,512]{2,1,0:T(8,128)}, f32[512,512]{1,0:T(8,128)}, f32[512,2048]{1,0:T(8,128)}, f32[2048,512]{1,0:T(8,128)}, bf16[4,256,512]{2,1,0:T...) custom-call(bf16[3,512,512]{2,1,0:T(8,128)(2,1)} %lq.1, ...), custom_call_target="tpu_custom_call" | custom-call | tf_op jit(solution)/shard_map/latent_grads/pallas_call | solution.py:1744
where the time goes:
time: 271 us; the launch traced here: 268 us
  Pallas kernels  267 us (99%)
    pallas_call x1, Pallas kernels, attention_back(): pl.pallas_call(functools.partial(backward_kernel, streams, groups, tile,...  104 us
    pallas_call x2, Pallas kernels, attention(): pl.pallas_call(functools.partial(forward_kernel, moves, keep, streams, gr...  78.1 us
    pallas_call x1, Pallas kernels, middle(): pl.pallas_call(functools.partial(middle_kernel, streams, groups, bag, til...  37.9 us
    pallas_call x1, Pallas kernels, intake(): pl.pallas_call(functools.partial(intake_kernel, moves, groups), out_shape...  33.2 us
    pallas_call x1, Pallas kernels, latent_grads(): pl.pallas_call(functools.partial(latent_grads_kernel, pairs, len(handed))...  14.1 us

commit v1 on v0

--- a/solution.py
+++ b/solution.py
@@ -553,8 +553,9 @@
             yield job, (source, target, *scratch[at : at + count])
             at += count
 
-    def first(self, sources, targets, scratch, count=None):
-        greet(unique(self.jobs + self.others))
+    def first(self, sources, targets, scratch, count=None, meet=True):
+        if meet:
+            greet(unique(self.jobs + self.others))
         for job, refs in list(self.each(sources, targets, scratch))[:count]:
             job.first(*refs)
 
@@ -584,87 +585,103 @@
     return (scale * jnp.tanh(matrix * (2.0 / scale))).astype(BF)
 
 
-def intake_kernel(moves, groups, *refs):
-    count = len(moves.jobs)
-    latents, ids_ref, refs = refs[:4], refs[4], refs[5:]
-    sources, refs = refs[: count - 1], refs[count - 1 :]
-    results, refs = refs[:4], refs[4:]
-    targets, refs = refs[:count], refs[count:]
-    loaded, made, sems = refs[:4], refs[4:8], refs[8]
-    ids_in, ids_box, *scratch = refs[9:]
-    sources = (*sources, ids_box)
-    moves.first(sources, targets, scratch, count - 1)
-    s, r = place(groups)
-    width = results[0].shape[3]
-    own = pl.ds(pl.multiple_of(r * width, 128), width)
-    places = [latents[0].at[:, :, own], *latents[1:]]
-    loads = [
-        pltpu.make_async_copy(source, target, sems.at[i])
-        for i, (source, target) in enumerate(zip(places, loaded))
-    ]
-    stores = [
-        pltpu.make_async_copy(source, target, sems.at[4 + i])
-        for i, (source, target) in enumerate(zip(made, [results[0].at[0], *results[1:]]))
-    ]
-    fetch = pltpu.make_async_copy(ids_ref, ids_in, sems.at[8])
-    fetch.start()
-    for copy in loads:
-        copy.start()
-    fetch.wait()
-    ids = ids_in[...].astype(F32)
-    for i in range(ids.shape[0]):
-        ids_box[i] = jnp.broadcast_to(ids[i : i + 1, :], ids_box.shape[1:])
-    moves.start_last(sources, targets, scratch)
-    loads[0].wait()
-    for i in range(3):
-        made[0][i] = binary_columns(loaded[0][i])
-    stores[0].start()
-    for n in range(1, 4):
-        loads[n].wait()
-        for i in range(0, loaded[n].shape[1], 128):
-            made[n][:, i : i + 128] = binary_columns(loaded[n][:, i : i + 128])
-        stores[n].start()
-    moves.middle(sources, targets, scratch)
-    for copy in stores:
-        copy.wait()
-    moves.last(sources, targets, scratch)
-
-
-def intake(moves, groups, latents, ids, arrays, collective_id):
-    three, depth, unused = latents[0].shape
-    own_shape = (three, depth, depth // groups)
-    shapes = [(1,) + own_shape] + [a.shape for a in latents[1:]]
-    buffers = [pltpu.VMEM(shape, BF) for shape in [own_shape] + shapes[1:]]
-    any_space = [pl.BlockSpec(memory_space=pl.ANY)] * 4
-    return pl.pallas_call(
-        functools.partial(intake_kernel, moves, groups),
-        out_shape=[jax.ShapeDtypeStruct(shape, BF) for shape in shapes] + moves.out_shapes(),
-        in_specs=any_space
-        + moves.spaces(),
-        out_specs=any_space + moves.spaces(),
-        scratch_shapes=buffers * 2
-        + [dma(9), pltpu.VMEM(ids.shape, ids.dtype)]
-        + [pltpu.VMEM((ids.shape[0], 8, ids.shape[1]), F32)]
-        + moves.scratch(),
-        compiler_params=remote_params(collective_id),
-        name="intake",
-    )(*latents, ids, *arrays)
+class Intake:
+    def __init__(self, bag, moves, groups, latents, ids, seq):
+        three, depth, unused = latents[0].shape
+        own = (three, depth, depth // groups)
+        self.moves, self.groups = moves, groups
+        self.shapes = [(1,) + own] + [a.shape for a in latents[1:]]
+        self.blocks = [job.out_shape() for job in moves.jobs]
+        for i, shape in enumerate(self.shapes):
+            bag.add(f"loaded{i}", pltpu.VMEM(own if i == 0 else shape, BF))
+            bag.add(f"made{i}", pltpu.VMEM(shape, BF))
+        bag.add("weight_sems", dma(4))
+        bag.add("made_sems", dma(4))
+        bag.add("in_sems", dma(3))
+        bag.add("ids_in", pltpu.VMEM(ids.shape, ids.dtype))
+        bag.add("ids_box", pltpu.VMEM((ids.shape[0], 8, ids.shape[1]), F32))
+        bag.add("x_all", pltpu.VMEM(self.blocks[0].shape, BF))
+        bag.add("docs", pltpu.VMEM(self.blocks[-1].shape, F32))
+        for i, item in enumerate(moves.scratch()):
+            bag.add(f"early{i}", item)
+
+    def run(self, have, latents, ids_ref, sources, results, targets, begin):
+        moves = self.moves
+        scratch = [have[f"early{i}"] for i in range(len(moves.scratch()))]
+        loaded = [have[f"loaded{i}"] for i in range(4)]
+        made = [have[f"made{i}"] for i in range(4)]
+        sources = (*sources, have["ids_box"])
+        moves.first(sources, targets, scratch, len(sources) - 1, False)
+        s, r = place(self.groups)
+        width = results[0].shape[3]
+        own = pl.ds(pl.multiple_of(r * width, 128), width)
+        places = [latents[0].at[:, :, own], *latents[1:]]
+        loads = [
+            pltpu.make_async_copy(places[i], loaded[i], have["weight_sems"].at[i])
+            for i in range(4)
+        ]
+        stores = [
+            pltpu.make_async_copy(made[i], results[i], have["made_sems"].at[i]) for i in range(4)
+        ]
+        fetch = pltpu.make_async_copy(ids_ref, have["ids_in"], have["in_sems"].at[0])
+        fetch.start()
+        for copy in loads:
+            copy.start()
+        fetch.wait()
+        ids = have["ids_in"][...].astype(F32)
+        for i in range(ids.shape[0]):
+            have["ids_box"][i] = jnp.broadcast_to(ids[i : i + 1, :], have["ids_box"].shape[1:])
+        moves.start_last(sources, targets, scratch)
+        loads[0].wait()
+        for i in range(3):
+            made[0][0, i] = binary_columns(loaded[0][i])
+        stores[0].start()
+        for n in range(1, 4):
+            loads[n].wait()
+            for i in range(0, loaded[n].shape[1], 128):
+                made[n][:, i : i + 128] = binary_columns(loaded[n][:, i : i + 128])
+            stores[n].start()
+        moves.middle(sources, targets, scratch)
+        for copy in stores:
+            copy.wait()
+        moves.last(sources, targets, scratch)
+        begin()
+        inward = [
+            pltpu.make_async_copy(targets[0], have["x_all"], have["in_sems"].at[1]),
+            pltpu.make_async_copy(targets[-1], have["docs"], have["in_sems"].at[2]),
+        ]
+        for copy in inward:
+            copy.start()
+        for copy in inward:
+            copy.wait()
 
 
 def lanes_of(shape):
     return lax.broadcasted_iota(jnp.int32, shape, 1)
 
 
-def forward_kernel(
-    moves, keep, streams, groups, tile, bag, tiles, x_ref, w_ref, bias_ref, docs_ref, *rest
-):
+def forward_kernel(intake, moves, streams, groups, tile, bag, tiles, *refs):
+    keep = intake is not None
+    refs = list(refs)
+
+    def take(n):
+        return [refs.pop(0) for unused in range(n)]
+
     count = len(moves.jobs)
-    sources, rest = rest[:count], rest[count:]
-    q_ref, k_ref, rows_ref, *rest = rest
     if keep:
-        v_ref, e_ref, ctx_ref, inv_ref, active_ref, *rest = rest
-    targets, rest = rest[:count], rest[count:]
-    have = bag.bind(rest)
+        (bias_ref,), latents, (ids_ref,) = take(1), take(4), take(1)
+        early_sources = take(len(intake.moves.jobs) - 1)
+    else:
+        x_ref, w_ref, bias_ref, docs_ref = take(4)
+    sources = take(count)
+    q_ref, k_ref, rows_ref = take(3)
+    if keep:
+        v_ref, e_ref, ctx_ref, inv_ref, active_ref = take(5)
+        results, early_targets = take(4), take(len(intake.moves.jobs))
+    targets = take(count)
+    have = bag.bind(refs)
+    if keep:
+        w_ref, docs_ref = have["made0"], have["docs"]
     scratch = tuple(have[f"moves{i}"] for i in range(len(moves.scratch())))
     k_aug, v_aug, ctx_all, mask, edges = (
         have["k_aug"],
@@ -688,7 +705,15 @@
 
     @pl.when((pair == 0) & (step == 0))
     def _():
-        moves.first(sources, targets, scratch)
+        if keep:
+            greet(unique(intake.moves.jobs + moves.jobs + moves.others))
+
+            def begin():
+                moves.first(sources, targets, scratch, None, False)
+
+            intake.run(have, latents, ids_ref, early_sources, results, early_targets, begin)
+        else:
+            moves.first(sources, targets, scratch)
         ids = stream_row(docs_ref)
         row_ref[...] = ids
         big_at = long_at(streams, groups, seq)
@@ -697,8 +722,11 @@
         edges[0] = jnp.broadcast_to(ids[:, :sub], (128, sub)).T
         edges[1] = jnp.broadcast_to(ids[:, seq - sub :], (128, sub)).T
         if keep:
-            for i in range(0, seq, 256):
-                active_ref[i : i + 256, :] = squash(x_ref[i : i + 256, :].astype(F32)).astype(BF)
+            x_all = have["x_all"]
+            shard = x_all.shape[1]
+            for i in range(x_all.shape[0]):
+                piece = squash(x_all[i].astype(F32)).astype(BF)
+                active_ref[i * shard : (i + 1) * shard, :] = piece
 
     @pl.when((pair == pairs - 1) & (step == steps - 2))
     def _():
@@ -833,8 +861,9 @@
     return streams * shard if groups > 1 else shard
 
 
-def attention(x, weights, bias, docs, streams, groups, moves, moved, keep, collective_id, name):
-    seq, depth = x.shape
+def attention(operands, seq, streams, groups, early, moves, moved, collective_id, name):
+    keep = early is not None
+    depth = operands[0].shape[-1]
     width = depth // groups
     pairs = width // 128
     tile = 512
@@ -849,6 +878,7 @@
     tiles = Tiles(bag, "tiles", groups, pairs, owned // tile)
     for i, item in enumerate(moves.scratch()):
         bag.add(f"moves{i}", item)
+    intake = Intake(bag, early, groups, operands[1:5], operands[5], seq) if keep else None
 
     def constant(shape):
         return pl.BlockSpec(shape, lambda p, i: (0,) * len(shape))
@@ -862,7 +892,9 @@
     wide = jax.ShapeDtypeStruct((seq, width), BF)
     outs = [whole, whole, any_space]
     shapes = [wide, wide, jax.ShapeDtypeStruct((groups, pairs, owned, 128), BF)]
+    ins = [constant(a.shape) for a in operands]
     if keep:
+        ins = ins[:1] + [any_space] * (len(operands) - 1)
         outs += [
             whole,
             pl.BlockSpec((2, tile, seq), lambda p, i: (p, turn(i), 0)),
@@ -870,6 +902,7 @@
             part,
             constant((seq, depth)),
         ]
+        outs += [any_space] * (4 + len(early.jobs))
         shapes += [
             wide,
             jax.ShapeDtypeStruct((2 * pairs, seq, seq), BF),
@@ -877,17 +910,17 @@
             jax.ShapeDtypeStruct((seq, width), F32),
             jax.ShapeDtypeStruct((seq, depth), BF),
         ]
+        shapes += [jax.ShapeDtypeStruct(shape, BF) for shape in intake.shapes] + intake.blocks
     return pl.pallas_call(
-        functools.partial(forward_kernel, moves, keep, streams, groups, tile, bag, tiles),
+        functools.partial(forward_kernel, intake, moves, streams, groups, tile, bag, tiles),
         grid=(pairs, seq // tile),
-        in_specs=[constant(a.shape) for a in (x, weights, bias, docs)]
-        + moves.spaces(),
+        in_specs=ins + moves.spaces(),
         out_specs=outs + moves.spaces(),
         out_shape=shapes + moves.out_shapes(),
         scratch_shapes=list(bag.items.values()),
         compiler_params=remote_params(collective_id),
         name=name,
-    )(x, weights, bias, docs, *moved)
+    )(*operands, *moved)
 
 
 def split(matrix):
@@ -1784,19 +1817,6 @@
     rows = seq // groups
     block = (shard_len, depth)
     gather, swap = Gather(streams, groups, block, BF), Swap(streams, groups, block, BF)
-    bin_own, bin_out, bin_up, bin_down, token_blocks, qkv_parts, docs = intake(
-        Moves(
-            gather,
-            Spread(teacher_qkv.shape, BF),
-            Gather(streams, groups, (8, shard_len), F32),
-        ),
-        groups,
-        [latent_qkv, latent_out, latent_up, latent_down],
-        segment_ids,
-        [tokens, teacher_qkv],
-        1,
-    )
-    stream_tokens = token_blocks.reshape(seq, depth)
     (
         queries,
         keys,
@@ -1806,33 +1826,50 @@
         context,
         inverse,
         active,
+        bin_own,
+        bin_out,
+        bin_up,
+        bin_down,
+        token_blocks,
+        qkv_parts,
+        docs,
         teacher_blocks,
         up_parts,
         out_parts,
     ) = attention(
-        stream_tokens,
-        bin_own,
-        student_bias,
-        docs,
+        [
+            student_bias,
+            latent_qkv,
+            latent_out,
+            latent_up,
+            latent_down,
+            segment_ids,
+            tokens,
+            teacher_qkv,
+        ],
+        seq,
         streams,
         groups,
+        Moves(
+            gather,
+            Spread(teacher_qkv.shape, BF),
+            Gather(streams, groups, (8, shard_len), F32),
+        ),
         Moves(gather, Spread(teacher_up.shape, BF), Spread(teacher_out.shape, BF)),
         [teacher_tokens, teacher_up, teacher_out],
-        True,
         2,
         "attention_student",
     )
+    stream_tokens = token_blocks.reshape(seq, depth)
     teacher_stream = teacher_blocks.reshape(seq, depth)
     teacher_queries, teacher_keys, tctx_rows, cot_blocks, down_parts = attention(
-        teacher_stream,
-        qkv_parts,
-        teacher_bias,
-        docs,
+        [teacher_stream, qkv_parts, teacher_bias, docs],
+        seq,
         streams,
         groups,
+        None,
         Moves(swap, Spread(teacher_down.shape, BF), others=[gather]),
         [cotangent, teacher_down],
-        False,
         3,
         "attention_teacher",
     )

time: 271 us -> 283 us (1.044)
  Pallas kernels: 267 us -> 278 us
    pallas_call x3 -> x2, Pallas kernels: 111 us -> 122 us  [attention(): pl.pallas_call(functools.partial(forward_kernel, intake, moves, streams,...]
where the time goes in v1:
time: 283 us; the launch traced here: 279 us
  Pallas kernels  278 us (98%)
    pallas_call x2, Pallas kernels, attention(): pl.pallas_call(functools.partial(forward_kernel, intake, moves, streams,...  122 us
    pallas_call x1, Pallas kernels, attention_back(): pl.pallas_call(functools.partial(backward_kernel, streams, groups, tile,...  104 us
    pallas_call x1, Pallas kernels, middle(): pl.pallas_call(functools.partial(middle_kernel, streams, groups, bag, til...  37.9 us
    pallas_call x1, Pallas kernels, latent_grads(): pl.pallas_call(functools.partial(latent_grads_kernel, pairs, len(handed))...  14.1 us

profile of v1, /device:TPU:0, one launch (start us, length us, event | category | flops | bytes accessed | tf_op | source)
XLA Modules:
  0.0 278.8 jit_solution(16148663559339178937)
XLA Ops:
  0.6 86.0 %attention_student.1 = (bf16[2048,256]{1,0:T(8,128)(2,1)}, bf16[2048,256]{1,0:T(8,128)(2,1)}, bf16[2,2,1024,128]{3,2,1,0:T(8,128)(2,1)}, bf16[2048,256]{1,0:T(8,...) custom-call(f32[6,512]{1,0:T(8,128)} %sb_ref.1, ...), custom_call_target="tpu_custom_call" | custom-call | tf_op jit(solution)/shard_map/attention_student/pallas_call | solution.py:914
  86.7 35.6 %attention_teacher.1 = (bf16[2048,256]{1,0:T(8,128)(2,1)}, bf16[2048,256]{1,0:T(8,128)(2,1)}, bf16[2,2,1024,128]{3,2,1,0:T(8,128)(2,1)}, bf16[4,256,512]{2,1,0:T(8,128)(2,1)}, bf16[4,512,512]{2,1,0:T(8,128)(2,1)}) custom-call(bf16[2048,512]{1,0:T(8,128)(2,1)} %bitcast.18, bf16[4,3,128,512]{3,2,1,0:T(8,128)(2,1)} %get-tuple-element.62.refs_1_, ...), custom_call_target="tpu_custom_call" | custom-call | tf_op jit(solution)/shard_map/attention_teacher/pallas_call | solution.py:914
  122.3 37.9 %middle.1 = (bf16[4,256,512]{2,1,0:T(8,128)(2,1)}, f32[1024,512]{1,0:T(8,128)}, bf16[2048,256]{1,0:T(8,128)(2,1)}, bf16[512,512]{1,0:T(8,128)(2,1)}, bf16[512,20...) custom-call(bf16[2048,512]{1,0:T(8,128)(2,1)} %bitcast.17, bf16[2048,512]{1,0:T(8,128)(2,1)} %bitcast.19, ...), custom_call_target="tpu_custom_call" | custom-call | tf_op jit(solution)/shard_map/middle/pallas_call | solution.py:1705
  160.2 104.2 %attention_back.1 = (bf16[4,256,512]{2,1,0:T(8,128)(2,1)}, bf16[2,4,4,16,2048]{4,3,2,1,0:T(8,128)(2,1)}, bf16[2,4,4,64,512]{4,3,2,1,0:T(8,128)(2,1)}, bf16[2,4,4...) custom-call(bf16[4,2048,2048]{2,1,0:T(8,128)(2,1)} %get-tuple-elemen, ...), custom_call_target="tpu_custom_call" | custom-call | tf_op jit(solution)/shard_map/attention_back/pallas_call | solution.py:1396
  264.5 14.1 %latent_grads.1 = (f32[3,512,512]{2,1,0:T(8,128)}, f32[512,512]{1,0:T(8,128)}, f32[512,2048]{1,0:T(8,128)}, f32[2048,512]{1,0:T(8,128)}, bf16[4,256,512]{2,1,0:T...) custom-call(bf16[3,512,512]{2,1,0:T(8,128)(2,1)} %lq.1, ...), custom_call_target="tpu_custom_call" | custom-call | tf_op jit(solution)/shard_map/latent_grads/pallas_call | solution.py:1777

commit v2 on v0

--- a/solution.py
+++ b/solution.py
@@ -673,7 +673,7 @@
         have["mask"],
         have["edges"],
     )
-    active = active_ref if keep else x_ref
+    active = have["active"] if keep else x_ref
     row_ref = have["row"]
     pair, step = pl.program_id(0), pl.program_id(1)
     pairs, steps = pl.num_programs(0), pl.num_programs(1)
@@ -698,7 +698,8 @@
         edges[1] = jnp.broadcast_to(ids[:, seq - sub :], (128, sub)).T
         if keep:
             for i in range(0, seq, 256):
-                active_ref[i : i + 256, :] = squash(x_ref[i : i + 256, :].astype(F32)).astype(BF)
+                active[i : i + 256, :] = squash(x_ref[i : i + 256, :].astype(F32)).astype(BF)
+            pltpu.make_async_copy(active, active_ref, have["active_sem"].at[0]).start()
 
     @pl.when((pair == pairs - 1) & (step == steps - 2))
     def _():
@@ -816,6 +817,8 @@
     def _():
         tiles.finish(have, source, target)
         moves.last(sources, targets, scratch)
+        if keep:
+            pltpu.make_async_copy(active, active_ref, have["active_sem"].at[0]).wait()
 
 
 def own_rows_last(step, seq, tile, groups):
@@ -845,6 +848,9 @@
     bag.add("ctx_all", pltpu.VMEM((pairs, seq, 128), BF))
     bag.add("mask", pltpu.VMEM((1, seq), F32))
     bag.add("row", pltpu.VMEM((1, seq), F32))
+    if keep:
+        bag.add("active", pltpu.VMEM((seq, depth), BF))
+        bag.add("active_sem", dma(1))
     bag.add("edges", pltpu.VMEM((2, 256, 128), F32))
     tiles = Tiles(bag, "tiles", groups, pairs, owned // tile)
     for i, item in enumerate(moves.scratch()):
@@ -868,7 +874,7 @@
             pl.BlockSpec((2, tile, seq), lambda p, i: (p, turn(i), 0)),
             part,
             part,
-            constant((seq, depth)),
+            any_space,
         ]
         shapes += [
             wide,
@@ -1615,6 +1621,15 @@
         small_ref[i : i + 1, :] += total(value)
     @pl.when(step == steps - 1)
     def _():
+        writes = []
+        for i, (total_ref, target) in enumerate(
+            ((gdown_acc, gdown_ref), (gup_acc, gup_ref), (gout_acc, gout_ref))
+        ):
+            narrow = have[f"narrow{i}"]
+            narrow[...] = total_ref[...].astype(BF)
+            copy = pltpu.make_async_copy(narrow, target, have["narrow_sems"].at[i])
+            copy.start()
+            writes.append(copy)
         tiles.finish(have, d_box.at[0, 0], dctx_ref.at[place_rows])
         source = out_box.at[0, pl.ds(0, shard)]
         pltpu.make_async_copy(source, out_ref.at[s], have["out_s"].at[s]).wait()
@@ -1623,9 +1638,8 @@
             remote(
                 source, out_ref.at[block], have["out_s"].at[block], have["out_r"].at[block], peer
             ).wait()
-        gout_ref[...] = gout_acc[...].astype(BF)
-        gup_ref[...] = gup_acc[...].astype(BF)
-        gdown_ref[...] = gdown_acc[...].astype(BF)
+        for copy in writes:
+            copy.wait()
 
 
 def row_tile(step, steps, streams, groups):
@@ -1664,6 +1678,9 @@
         bag.add(f"weight{2 * i}", pltpu.VMEM(teacher_weights[i].shape, BF))
         bag.add(f"weight{2 * i + 1}", pltpu.VMEM(weights[i].shape, BF))
     bag.add("weight_sems", dma(6))
+    for i in range(3):
+        bag.add(f"narrow{i}", pltpu.VMEM(out_full[2 - i], BF))
+    bag.add("narrow_sems", dma(3))
     bag.add("out_box", pltpu.VMEM((steps, tile, depth), BF))
     bag.add("d_box", pltpu.VMEM((steps, groups, tile, width), BF))
     bag.add("out_s", dma(streams))
@@ -1675,7 +1692,7 @@
         in_specs=[of_stream, of_stream, tall, split_rows, split_rows]
         + [any_space] * 6
         + [full(a.shape) for a in vectors],
-        out_specs=[any_space, tall, any_space] + [full(s) for s in out_full],
+        out_specs=[any_space, tall, any_space] + [any_space] * 3 + [full(out_full[3])],
         out_shape=[
             jax.ShapeDtypeStruct((streams, shard, depth), BF),
             jax.ShapeDtypeStruct((rows, depth), F32),

time: 271 us -> 270 us (level)
  no operation moved by 1% of the time
where the time goes in v2:
time: 270 us; the launch traced here: 266 us
  Pallas kernels  265 us (98%)
    pallas_call x1, Pallas kernels, attention_back(): pl.pallas_call(functools.partial(backward_kernel, streams, groups, tile,...  103 us
    pallas_call x2, Pallas kernels, attention(): pl.pallas_call(functools.partial(forward_kernel, moves, keep, streams, gr...  77.5 us
    pallas_call x1, Pallas kernels, middle(): pl.pallas_call(functools.partial(middle_kernel, streams, groups, bag, til...  37.2 us
    pallas_call x1, Pallas kernels, intake(): pl.pallas_call(functools.partial(intake_kernel, moves, groups), out_shape...  33.2 us
    pallas_call x1, Pallas kernels, latent_grads(): pl.pallas_call(functools.partial(latent_grads_kernel, pairs, len(handed))...  14.1 us

profile of v2, /device:TPU:0, one launch (start us, length us, event | category | flops | bytes accessed | tf_op | source)
XLA Modules:
  0.0 265.5 jit_solution(1357732474805764520)
XLA Ops:
  0.6 33.2 %intake.1 = (bf16[1,3,512,256]{3,2,1,0:T(8,128)(2,1)}, bf16[512,512]{1,0:T(8,128)(2,1)}, bf16[512,2048]{1,0:T(8,128)(2,1)}, bf16[2048,512]{1,0:T(8,128)(2,1)}, b...) custom-call(bf16[3,512,512]{2,1,0:T(8,128)(2,1)} %lq.1, bf16[512,512]{1,0:T(8,128)(2,1)} %lo.1, ...), custom_call_target="tpu_custom_call" | custom-call | tf_op jit(solution)/shard_map/intake/pallas_call | solution.py:639
  33.8 40.5 %attention_student.1 = (bf16[2048,256]{1,0:T(8,128)(2,1)}, bf16[2048,256]{1,0:T(8,128)(2,1)}, bf16[2,2,1024,128]{3,2,1,0:T(8,128)(2,1)}, bf16[2048,256]{1,0:T(8,...) custom-call(bf16[2048,512]{1,0:T(8,128)(2,1)} %bitcast.17, ...), custom_call_target="tpu_custom_call" | custom-call | tf_op jit(solution)/shard_map/attention_student/pallas_call | solution.py:886
  74.4 37.0 %attention_teacher.1 = (bf16[2048,256]{1,0:T(8,128)(2,1)}, bf16[2048,256]{1,0:T(8,128)(2,1)}, bf16[2,2,1024,128]{3,2,1,0:T(8,128)(2,1)}, bf16[4,256,512]{2,1,0:T(8,128)(2,1)}, bf16[4,512,512]{2,1,0:T(8,128)(2,1)}) custom-call(bf16[2048,512]{1,0:T(8,128)(2,1)} %bitcast.19, bf16[4,3,128,512]{3,2,1,0:T(8,128)(2,1)} %get-tuple-element.65.w_ref, ...), custom_call_target="tpu_custom_call" | custom-call | tf_op jit(solution)/shard_map/attention_teacher/pallas_call | solution.py:886
  111.3 37.2 %middle.1 = (bf16[4,256,512]{2,1,0:T(8,128)(2,1)}, f32[1024,512]{1,0:T(8,128)}, bf16[2048,256]{1,0:T(8,128)(2,1)}, bf16[512,512]{1,0:T(8,128)(2,1)}, bf16[512,20...) custom-call(bf16[2048,512]{1,0:T(8,128)(2,1)} %bitcast.18, bf16[2048,512]{1,0:T(8,128)(2,1)} %bitcast.20, ...), custom_call_target="tpu_custom_call" | custom-call | tf_op jit(solution)/shard_map/middle/pallas_call | solution.py:1689
  148.6 102.6 %attention_back.1 = (bf16[4,256,512]{2,1,0:T(8,128)(2,1)}, bf16[2,4,4,16,2048]{4,3,2,1,0:T(8,128)(2,1)}, bf16[2,4,4,64,512]{4,3,2,1,0:T(8,128)(2,1)}, bf16[2,4,4...) custom-call(bf16[4,2048,2048]{2,1,0:T(8,128)(2,1)} %get-tuple-elemen, ...), custom_call_target="tpu_custom_call" | custom-call | tf_op jit(solution)/shard_map/attention_back/pallas_call | solution.py:1369
  251.1 14.1 %latent_grads.1 = (f32[3,512,512]{2,1,0:T(8,128)}, f32[512,512]{1,0:T(8,128)}, f32[512,2048]{1,0:T(8,128)}, f32[2048,512]{1,0:T(8,128)}, bf16[4,256,512]{2,1,0:T...) custom-call(bf16[3,512,512]{2,1,0:T(8,128)(2,1)} %lq.1, ...), custom_call_target="tpu_custom_call" | custom-call | tf_op jit(solution)/shard_map/latent_grads/pallas_call | solution.py:1761

commit v3 on v2

--- a/solution.py
+++ b/solution.py
@@ -660,9 +660,9 @@
 ):
     count = len(moves.jobs)
     sources, rest = rest[:count], rest[count:]
-    q_ref, k_ref, rows_ref, *rest = rest
+    q_out, k_out, rows_ref, *rest = rest
     if keep:
-        v_ref, e_ref, ctx_ref, inv_ref, active_ref, *rest = rest
+        v_out, e_ref, ctx_ref, inv_ref, active_ref, *rest = rest
     targets, rest = rest[:count], rest[count:]
     have = bag.bind(rest)
     scratch = tuple(have[f"moves{i}"] for i in range(len(moves.scratch())))
@@ -677,7 +677,18 @@
     row_ref = have["row"]
     pair, step = pl.program_id(0), pl.program_id(1)
     pairs, steps = pl.num_programs(0), pl.num_programs(1)
-    seq = k_ref.shape[0]
+    seq = k_aug.shape[1]
+    kept = have["kept"]
+    q_ref, k_ref = kept.at[0, pair], kept.at[1, pair]
+    outputs = [q_out, k_out, v_out] if keep else [q_out, k_out]
+
+    def writes(p):
+        columns = pl.ds(pl.multiple_of(p * 128, 128), 128)
+        return [
+            pltpu.make_async_copy(kept.at[i, p], target.at[:, columns], have["kept_sems"].at[i, p])
+            for i, target in enumerate(outputs)
+        ]
+
     s, r = place(groups)
     sub = min(256, tile)
     width = w_ref.shape[3]
@@ -729,7 +740,9 @@
         k_aug[1] = jnp.where(low, turned, keys).astype(BF)
         values = project(2, 1)
         if keep:
-            v_ref[...] = values
+            kept[2, pair] = values
+        for copy in writes(pair):
+            copy.start()
         values = values.astype(F32)
         v_aug[0] = jnp.where(low, values, jnp.where(lane < 66, 1.0, 0.0)).astype(BF)
         v_aug[1] = jnp.where(low, jnp.where(lane < 2, 1.0, 0.0), values).astype(BF)
@@ -817,6 +830,9 @@
     def _():
         tiles.finish(have, source, target)
         moves.last(sources, targets, scratch)
+        for p in range(n_pairs):
+            for copy in writes(p):
+                copy.wait()
         if keep:
             pltpu.make_async_copy(active, active_ref, have["active_sem"].at[0]).wait()
 
@@ -848,6 +864,8 @@
     bag.add("ctx_all", pltpu.VMEM((pairs, seq, 128), BF))
     bag.add("mask", pltpu.VMEM((1, seq), F32))
     bag.add("row", pltpu.VMEM((1, seq), F32))
+    bag.add("kept", pltpu.VMEM((3 if keep else 2, pairs, seq, 128), BF))
+    bag.add("kept_sems", pltpu.SemaphoreType.DMA((3, pairs)))
     if keep:
         bag.add("active", pltpu.VMEM((seq, depth), BF))
         bag.add("active_sem", dma(1))
@@ -863,14 +881,13 @@
         return own_rows_last(i, seq, tile, groups)
 
     part = pl.BlockSpec((tile, 128), lambda p, i: (turn(i), p))
-    whole = pl.BlockSpec((seq, 128), lambda p, i: (0, p))
     any_space = pl.BlockSpec(memory_space=pl.ANY)
     wide = jax.ShapeDtypeStruct((seq, width), BF)
-    outs = [whole, whole, any_space]
+    outs = [any_space, any_space, any_space]
     shapes = [wide, wide, jax.ShapeDtypeStruct((groups, pairs, owned, 128), BF)]
     if keep:
         outs += [
-            whole,
+            any_space,
             pl.BlockSpec((2, tile, seq), lambda p, i: (p, turn(i), 0)),
             part,
             part,

time: 270 us -> 268 us (level)
  no operation moved by 1% of the time
where the time goes in v3:
time: 268 us; the launch traced here: 264 us
  Pallas kernels  264 us (99%)
    pallas_call x1, Pallas kernels, attention_back(): pl.pallas_call(functools.partial(backward_kernel, streams, groups, tile,...  103 us
    pallas_call x2, Pallas kernels, attention(): pl.pallas_call(functools.partial(forward_kernel, moves, keep, streams, gr...  76 us
    pallas_call x1, Pallas kernels, middle(): pl.pallas_call(functools.partial(middle_kernel, streams, groups, bag, til...  37.1 us
    pallas_call x1, Pallas kernels, intake(): pl.pallas_call(functools.partial(intake_kernel, moves, groups), out_shape...  33.2 us
    pallas_call x1, Pallas kernels, latent_grads(): pl.pallas_call(functools.partial(latent_grads_kernel, pairs, len(handed))...  14.1 us

profile of v3, /device:TPU:0, one launch (start us, length us, event | category | flops | bytes accessed | tf_op | source)
XLA Modules:
  0.0 264.5 jit_solution(8806049301760069347)
XLA Ops:
  0.6 33.2 %intake.1 = (bf16[1,3,512,256]{3,2,1,0:T(8,128)(2,1)}, bf16[512,512]{1,0:T(8,128)(2,1)}, bf16[512,2048]{1,0:T(8,128)(2,1)}, bf16[2048,512]{1,0:T(8,128)(2,1)}, b...) custom-call(bf16[3,512,512]{2,1,0:T(8,128)(2,1)} %lq.1, bf16[512,512]{1,0:T(8,128)(2,1)} %lo.1, ...), custom_call_target="tpu_custom_call" | custom-call | tf_op jit(solution)/shard_map/intake/pallas_call | solution.py:639
  33.8 40.0 %attention_student.1 = (bf16[2048,256]{1,0:T(8,128)(2,1)}, bf16[2048,256]{1,0:T(8,128)(2,1)}, bf16[2,2,1024,128]{3,2,1,0:T(8,128)(2,1)}, bf16[2048,256]{1,0:T(8,...) custom-call(bf16[2048,512]{1,0:T(8,128)(2,1)} %bitcast.17, ...), custom_call_target="tpu_custom_call" | custom-call | tf_op jit(solution)/shard_map/attention_student/pallas_call | solution.py:903
  73.8 36.1 %attention_teacher.1 = (bf16[2048,256]{1,0:T(8,128)(2,1)}, bf16[2048,256]{1,0:T(8,128)(2,1)}, bf16[2,2,1024,128]{3,2,1,0:T(8,128)(2,1)}, bf16[4,256,512]{2,1,0:T(8,128)(2,1)}, bf16[4,512,512]{2,1,0:T(8,128)(2,1)}) custom-call(bf16[2048,512]{1,0:T(8,128)(2,1)} %bitcast.19, bf16[4,3,128,512]{3,2,1,0:T(8,128)(2,1)} %get-tuple-element.65.w_ref, ...), custom_call_target="tpu_custom_call" | custom-call | tf_op jit(solution)/shard_map/attention_teacher/pallas_call | solution.py:903
  109.9 37.1 %middle.1 = (bf16[4,256,512]{2,1,0:T(8,128)(2,1)}, f32[1024,512]{1,0:T(8,128)}, bf16[2048,256]{1,0:T(8,128)(2,1)}, bf16[512,512]{1,0:T(8,128)(2,1)}, bf16[512,20...) custom-call(bf16[2048,512]{1,0:T(8,128)(2,1)} %bitcast.18, bf16[2048,512]{1,0:T(8,128)(2,1)} %bitcast.20, ...), custom_call_target="tpu_custom_call" | custom-call | tf_op jit(solution)/shard_map/middle/pallas_call | solution.py:1706
  147.0 103.1 %attention_back.1 = (bf16[4,256,512]{2,1,0:T(8,128)(2,1)}, bf16[2,4,4,16,2048]{4,3,2,1,0:T(8,128)(2,1)}, bf16[2,4,4,64,512]{4,3,2,1,0:T(8,128)(2,1)}, bf16[2,4,4...) custom-call(bf16[4,2048,2048]{2,1,0:T(8,128)(2,1)} %get-tuple-elemen, ...), custom_call_target="tpu_custom_call" | custom-call | tf_op jit(solution)/shard_map/attention_back/pallas_call | solution.py:1386
  250.1 14.1 %latent_grads.1 = (f32[3,512,512]{2,1,0:T(8,128)}, f32[512,512]{1,0:T(8,128)}, f32[512,2048]{1,0:T(8,128)}, f32[2048,512]{1,0:T(8,128)}, bf16[4,256,512]{2,1,0:T...) custom-call(bf16[3,512,512]{2,1,0:T(8,128)(2,1)} %lq.1, ...), custom_call_target="tpu_custom_call" | custom-call | tf_op jit(solution)/shard_map/latent_grads/pallas_call | solution.py:1778
